TPU v7x, 128 devices: a whole 4x4x4 slice. The times are simulated.
128 devices in a mesh: ctx: 8 (over y, z_hi), sess: 16 (over z_lo, x, core).
Axes of the slice: x: 4, y: 4, z: 4 (z_hi: 2, z_lo: 2; z = z_hi * 2 + z_lo), core: 2. Of those that a mesh axis runs over, the one named last changes fastest.
Arguments:
- mel_in: bfloat16 [196608, 128], P(('ctx', 'sess')), may hold values from -6 to 6
- route: int32 [196608], P(('ctx', 'sess')), may hold values from 0 to 1535, as said below
- lengths: int32 [16], replicated, may hold values from 1 to 3072, 24576 in all
- conv_first: bfloat16 [9, 128], replicated, may hold values from -2 to 2
- conv_second: bfloat16 [1152, 128], replicated, may hold values from -0.1875 to 0.1875
- lin_in: bfloat16 [4096, 1536], replicated, may hold values from -0.1875 to 0.1875
- wq: bfloat16 [1536, 768], P('sess'), may hold values from -4.8989795 to 4.8989795
- wk: bfloat16 [1536, 768], P('sess'), may hold values from -0.15309311 to 0.15309311
- wv: bfloat16 [1536, 768], P('sess'), may hold values from -0.15625 to 0.15625
- wo: bfloat16 [768, 1536], P('sess'), may hold values from -0.21875 to 0.21875
- pw1: bfloat16 [1536, 3072], P('sess'), may hold values from -0.15625 to 0.15625
- dw_kernel: bfloat16 [31, 1536], replicated, may hold values from -1 to 1
Outputs:
- encoded: bfloat16 [16, 3072, 1536], P('sess', 'ctx')
Inputs may be any that keep to these rules, and one draw needn't show every extreme that they name: `route`: for each device j, the positions carried by the rows bound for j from all devices form a permutation of 0 to 1535.
All inputs are finite; a program needn't handle non-finite values.
Results may differ from a plain program's by a relative error of at most 0.014.
Values may be sent and summed in bfloat16 or wider, within the bound.
A program may use at most 192 MiB of HBM per device.

v0:
```python
import math

import jax
import jax.numpy as jnp
from jax import lax
from jax.sharding import PartitionSpec as P

HEADS = 8
HEAD = 96
KERNEL = 31


eps = 1e-05


def from_behind(block, axis, distance):
    devices = range(lax.axis_size(axis))
    route = [(i - distance, i) for i in devices if i - distance in devices]
    return lax.ppermute(block, axis, route)


def extended_2(block, sides, width):
    for axis, dim in sides:
        count = lax.axis_size(axis)
        forward = [(i, i + 1) for i in range(count - 1)]
        backward = [(target, source) for source, target in forward]
        low = lax.ppermute(
            lax.slice_in_dim(block, block.shape[dim] - width, None, axis=dim), axis, forward
        )
        high = lax.ppermute(lax.slice_in_dim(block, 0, width, axis=dim), axis, backward)
        block = jnp.concatenate([low, block, high], axis=dim)
    return block


def first_conv(padded, kernel):
    row_count = (padded.shape[0] - 1) // 2
    bin_count = padded.shape[1]
    half_bins = bin_count // 2
    channels = kernel.shape[1]
    paired = padded[: 2 * row_count].reshape(row_count, 2 * bin_count)
    next_rows = jnp.concatenate(
        [paired[1:, :bin_count], padded[2 * row_count : 2 * row_count + 1]], axis=0
    )
    patches = jnp.concatenate([paired, next_rows], axis=1)
    bin_index = jnp.arange(bin_count, dtype=jnp.int32)
    out_index = jnp.arange(half_bins, dtype=jnp.int32)
    select = jnp.stack(
        [bin_index[:, None] == 2 * out_index[None, :] + b - 1 for b in range(3)], axis=0
    ).astype(jnp.bfloat16)
    banded = jnp.einsum(
        "bmf,abc->amfc", select, kernel.reshape(3, 3, channels), preferred_element_type=jnp.float32
    )
    banded = banded.astype(jnp.bfloat16).reshape(3 * bin_count, half_bins * channels)
    running = jnp.dot(patches, banded, preferred_element_type=jnp.float32)
    return jnp.maximum(running, 0.0).astype(jnp.bfloat16).reshape(row_count, half_bins, channels)


def second_conv(padded, kernel):
    total_rows, bin_count, channels = padded.shape
    row_count = (total_rows - 1) // 2
    half_bins = bin_count // 2
    paired = padded.reshape(total_rows, half_bins, 2 * channels)
    left = jnp.concatenate(
        [jnp.zeros((total_rows, 1, channels), padded.dtype), paired[:, :-1, channels:]], axis=1
    )
    bin_taps = jnp.concatenate([left, paired], axis=2)
    row_pairs = bin_taps[: 2 * row_count].reshape(row_count, 2, half_bins, 3 * channels)
    third = jnp.concatenate([row_pairs[1:, 0], bin_taps[2 * row_count : 2 * row_count + 1]], axis=0)
    patches = jnp.concatenate([row_pairs[:, 0], row_pairs[:, 1], third], axis=2).reshape(
        row_count * half_bins, 9 * channels
    )
    running = jnp.dot(patches, kernel, preferred_element_type=jnp.float32)
    return jnp.maximum(running, 0.0).astype(jnp.bfloat16).reshape(row_count, half_bins * channels)


def layer_norm(rows_in):
    values = rows_in.astype(jnp.float32)
    row_mean = jnp.mean(values, axis=-1, keepdims=True)
    centred = values - row_mean
    variance = jnp.mean(centred * centred, axis=-1, keepdims=True)
    return (centred * lax.rsqrt(variance + eps)).astype(jnp.bfloat16)


def depthwise(extended, kernel, row_count):
    running = jnp.zeros((row_count, extended.shape[1]), jnp.float32)
    for j in range(kernel.shape[0]):
        running = (
            running
            + extended[j : j + row_count].astype(jnp.float32)
            * kernel[j].astype(jnp.float32)[None, :]
        )
    return running


def local(mel_in, route, lengths, conv_first, conv_second, lin_in, wq, wk, wv, wo, pw1, dw_kernel):
    rank_count = lax.axis_size("ctx") * lax.axis_size("sess")
    mel_rows, mel_width = mel_in.shape
    slot_rows = mel_rows // rank_count
    arrived, places = (
        lax.all_to_all(
            mel_in.reshape(rank_count, slot_rows, mel_width),
            ("ctx", "sess"),
            split_axis=0,
            concat_axis=0,
            tiled=True,
        ),
        lax.all_to_all(
            route.reshape(rank_count, slot_rows),
            ("ctx", "sess"),
            split_axis=0,
            concat_axis=0,
            tiled=True,
        ),
    )
    frames = (
        jnp.zeros((mel_rows, mel_width), mel_in.dtype)
        .at[places.reshape(mel_rows)]
        .set(arrived.reshape(mel_rows, mel_width))
    )
    mel_rim = from_behind(frames[-3:], "ctx", 1)
    first_out = first_conv(jnp.concatenate([mel_rim, frames], axis=0), conv_first)
    second_out = second_conv(first_out, conv_second)
    embedded = jnp.dot(second_out, lin_in, preferred_element_type=jnp.float32).astype(jnp.bfloat16)
    w_query, w_key, w_value, w_out, w_up = (
        lax.all_gather(wq, "sess", axis=0, tiled=True),
        lax.all_gather(wk, "sess", axis=0, tiled=True),
        lax.all_gather(wv, "sess", axis=0, tiled=True),
        lax.all_gather(wo, "sess", axis=0, tiled=True),
        lax.all_gather(pw1, "sess", axis=0, tiled=True),
    )
    normed = layer_norm(embedded)
    queries = jnp.dot(normed, w_query, preferred_element_type=jnp.float32).astype(jnp.bfloat16)
    key_rows = jnp.dot(normed, w_key, preferred_element_type=jnp.float32).astype(jnp.bfloat16)
    values = jnp.dot(normed, w_value, preferred_element_type=jnp.float32).astype(jnp.bfloat16)
    length = lengths[lax.axis_index("sess")]
    row_count = queries.shape[0]
    feature_count = embedded.shape[1]
    head_query = queries.reshape(row_count, HEADS, HEAD).transpose(1, 0, 2)
    score_scale = 1.0 / math.sqrt(HEAD)
    first_row = jnp.int32(0)
    row_max = jnp.full((HEADS, row_count), -1e30, jnp.float32)
    weight_sum = jnp.zeros((HEADS, row_count), jnp.float32)
    weighted_sum = jnp.zeros((HEADS, row_count, HEAD), jnp.float32)
    key_part = lax.all_gather(key_rows, "ctx", axis=0, tiled=True)
    value_part = lax.all_gather(values, "ctx", axis=0, tiled=True)
    piece_rows = key_part.shape[0]
    block_rows = math.gcd(piece_rows, 512)
    for offset in range(0, piece_rows, block_rows):
        key_block = key_part[offset : offset + block_rows].reshape(block_rows, HEADS, HEAD)
        value_block = value_part[offset : offset + block_rows].reshape(block_rows, HEADS, HEAD)
        is_valid = first_row + offset + jnp.arange(block_rows, dtype=jnp.int32) < length
        scores = (
            jnp.einsum("hqe,khe->hqk", head_query, key_block, preferred_element_type=jnp.float32)
            * score_scale
        )
        masked = jnp.where(is_valid[None, None, :], scores, -1e30)
        new_max = jnp.maximum(row_max, jnp.max(masked, axis=2))
        weights = jnp.where(
            is_valid[None, None, :], jnp.exp(scores - new_max[:, :, None]), 0.0
        ).astype(jnp.bfloat16)
        rescale = jnp.exp(row_max - new_max)
        weight_sum = weight_sum * rescale + jnp.sum(weights.astype(jnp.float32), axis=2)
        weighted_sum = weighted_sum * rescale[:, :, None] + jnp.einsum(
            "hqk,khe->hqe", weights, value_block, preferred_element_type=jnp.float32
        )
        row_max = new_max
    row_max, weight_sum, weighted_sum = (row_max, weight_sum, weighted_sum)
    context = (
        (weighted_sum / weight_sum[:, :, None])
        .transpose(1, 0, 2)
        .reshape(row_count, HEADS * HEAD)
        .astype(jnp.bfloat16)
    )
    residual = (
        embedded.astype(jnp.float32) + jnp.dot(context, w_out, preferred_element_type=jnp.float32)
    ).astype(jnp.bfloat16)
    normed_again = layer_norm(residual)
    lifted = jnp.dot(normed_again, w_up, preferred_element_type=jnp.float32)
    gated_rows = lifted[:, :feature_count] * jax.nn.sigmoid(lifted[:, feature_count:])
    position = lax.axis_index("ctx") * row_count + jnp.arange(row_count, dtype=jnp.int32)
    gated_rows = jnp.where((position < length)[:, None], gated_rows, 0.0).astype(jnp.bfloat16)
    extended = extended_2(gated_rows, (("ctx", 0),), KERNEL // 2)
    depth_out = depthwise(extended, dw_kernel, row_count)
    encoded = (residual.astype(jnp.float32) + depth_out * jax.nn.sigmoid(depth_out)).astype(
        jnp.bfloat16
    )
    return encoded[None]


def solution(mesh):
    return jax.shard_map(
        local,
        mesh=mesh,
        in_specs=(
            P(("ctx", "sess"), None),
            P(("ctx", "sess")),
            P(),
            P(),
            P(),
            P(),
            P("sess", None),
            P("sess", None),
            P("sess", None),
            P("sess", None),
            P("sess", None),
            P(),
        ),
        out_specs=P("sess", "ctx", None),
        check_vma=False,
    )
```

profile of v0, /device:TPU:0, one launch (start us, length us, event | category | flops | bytes accessed | tf_op | source)
XLA Modules:
  0.0 463.6 jit_solution(2322308828492838904)
XLA Ops:
  9.4 11.1 %all-to-all-start = ((s32[128,1,12]{2,1,0:T(1,128)}), s32[128,1,12]{2,1,0:T(1,128)S(1)}, u32[]{:S(2)}, u32[]{:S(2)}) async-start(s32[128,1,12]{2,1,0:T(1,128)} %bitcast), calls=%async_computation | async-start | bytes 131072 | tf_op jit(solution)/shard_map/all_to_all | solution.py:107
  23.4 6.6 %all-to-all-done = s32[128,1,12]{2,1,0:T(1,128)S(1)} async-done(((s32[128,1,12]{2,1,0:T(1,128)}), s32[128,1,12]{2,1,0:T(1,128)S(1)}, u32[]{:S(2)}, u32[]{:S(2)}) %all-to-all-start) | async-done | bytes 6176 | tf_op jit(solution)/shard_map/all_to_all | solution.py:107
  29.9 4.8 %all-to-all-start.1 = ((bf16[128,12,128]{2,1,0:T(8,128)(2,1)}), bf16[128,12,128]{2,1,0:T(8,128)(2,1)S(1)}, u32[]{:S(2)}, u32[]{:S(2)}) async-start(bf16[128,12,128]{2,1,0:T(8,128)(2,1)} %reshape.406), calls=%async_computation.1 | async-start | bytes 1048576 | tf_op jit(solution)/shard_map/all_to_all | solution.py:100
  36.7 14.6 %all-to-all-done.1 = bf16[128,12,128]{2,1,0:T(8,128)(2,1)S(1)} async-done(((bf16[128,12,128]{2,1,0:T(8,128)(2,1)}), bf16[128,12,128]{2,1,0:T(8,128)(2,1)S(1)}, u32[]{:S(2)}, u32[]{:S(2)}) %all-to-all-start.1) | async-done | bytes 393248 | tf_op jit(solution)/shard_map/all_to_all | solution.py:100
  51.4 4.6 scatter_custom_fusion
  60.5 6.7 %copy.41 = bf16[3,128,64,128]{3,2,1,0:T(8,128)(2,1)} copy(bf16[3,128,64,128]{3,1,0,2:T(8,128)(2,1)S(1)} %convert_bitcast_fusion) | data formatting | bytes 12582912 | tf_op jit(solution)/shard_map/convert_element_type | solution.py:53
  67.5 15.3 %maximum_convert_fusion = bf16[769,8192]{1,0:T(8,128)(2,1)} fusion(bf16[48,8,64,128]{3,2,1,0:T(8,128)(2,1)} %bitcast.211, bf16[1,128]{1,0:T(2,128)(2,1)S(1)} %slice.380, bf16[768,128]{1,0:T(8,128)(2,1)S(1)} %slice.379, bf16[769,256]{1,0:T(8,128)(2,1)S(1)} %reshape.408), kind=kOutput, calls=%fused_computation.9 | convolution fusion | flops 4852500480 | bytes 19481344 | tf_op jit(solution)/shard_map/dot_general | solution.py:54
  82.8 8.1 %copy.57 = bf16[97,8,32,256]{3,2,1,0:T(8,128)(2,1)S(1)} copy(bf16[97,8,32,256]{3,1,2,0:T(8,128)(2,1)} %bitcast.207) | data formatting | bytes 25427968
  90.8 5.7 %slice.459 = bf16[769,32,256]{2,1,0:T(8,128)(2,1)} slice(bf16[776,32,256]{2,1,0:T(8,128)(2,1)S(1)} %bitcast.197), slice={[0:769], [0:32], [0:256]} | slice | bytes 25198592 | tf_op jit(solution)/shard_map/reshape;reshape | solution.py:62
  98.1 9.9 %fusion.7 = bf16[769,32,384]{2,1,0:T(8,128)(2,1)S(1)} fusion(bf16[769,31,128]{2,1,0:T(8,128)(2,1)S(1)} %slice.381, bf16[769,32,256]{2,1,0:T(8,128)(2,1)} %slice.459), kind=kLoop, calls=%fused_computation.10 | loop fusion | flops 56696832 | bytes 37601024 | tf_op jit(solution)/shard_map/concatenate | solution.py:66
  108.0 12.2 %slice.382 = bf16[768,32,384]{2,1,0:T(8,128)(2,1)} slice(bf16[769,32,384]{2,1,0:T(8,128)(2,1)S(1)} %fusion.7), slice={[0:768], [0:32], [0:384]} | slice | bytes 37748736 | tf_op jit(solution)/shard_map/slice | solution.py:67
  120.3 8.3 %slice_bitcast_fusion = bf16[383,32,384]{2,1,0:T(8,128)(2,1)} fusion(bf16[384,2,32,384]{3,2,1,0:T(8,128)(2,1)} %bitcast.195), kind=kLoop, calls=%fused_computation.14 | loop fusion | bytes 18825216 | tf_op jit(solution)/shard_map/squeeze | solution.py:68
  128.6 15.0 %fusion.121 = (bf16[384,1,32,384]{3,2,1,0:T(8,128)(2,1)}, bf16[384,1,32,384]{3,2,1,0:T(8,128)(2,1)}) fusion(bf16[384,2,32,384]{3,2,1,0:T(8,128)(2,1)} %bitcast.196), kind=kLoop, calls=%fused_computation.267 | loop fusion | bytes 37748736 | tf_op jit(solution)/shard_map/slice | solution.py:69
  143.6 8.3 %pad_maximum_fusion = bf16[384,32,384]{2,1,0:T(8,128)(2,1)} fusion(bf16[1,32,384]{2,1,0:T(8,128)(2,1)S(1)} %slice-done, bf16[383,32,384]{2,1,0:T(8,128)(2,1)} %slice_bitcast_fusion), kind=kLoop, calls=%fused_computation.13 | loop fusion | flops 4718592 | bytes 18874368 | tf_op jit(solution)/shard_map/concatenate | solution.py:68
  152.0 13.1 %fusion.11 = bf16[12288,128]{1,0:T(8,128)(2,1)S(1)} fusion(bf16[1152,128]{1,0:T(8,128)(2,1)S(1)} %copy-done, bf16[12288,384]{1,0:T(8,128)(2,1)} %bitcast.208, bf16[12288,384]{1,0:T(8,128)(2,1)} %bitcast.210, bf16[12288,384]{1,0:T(8,128)(2,1)} %bitcast.209), kind=kOutput, calls=%fused_computation.12 | convolution fusion | flops 3711959040 | bytes 31752192 | tf_op jit(solution)/shard_map/dot_general | solution.py:72
  165.1 3.4 reshape.412
  168.5 9.2 %convert_reduce_fusion.7 = (f32[384]{0:T(512)S(1)}, bf16[384,1536]{1,0:T(8,128)(2,1)S(1)}) fusion(bf16[384,4096]{1,0:T(8,128)(2,1)} %reshape.412, bf16[4096,1536]{1,0:T(8,128)(2,1)} %param.17), kind=kOutput, calls=%fused_computation.69 | convolution fusion | flops 4833607168 | bytes 16909824 | tf_op jit(solution)/shard_map/dot_general | solution.py:123
  178.2 3.6 convolution_convert_fusion.2
  181.9 3.6 convolution_convert_fusion.1
  190.7 3.0 convolution_convert_fusion.3
  194.0 62.1 %all-gather.12.cloned.1.call-done = bf16[3072,768]{1,0:T(8,128)(2,1)} async-done(((bf16[384,768]{1,0:T(8,128)(2,1)}), bf16[3072,768]{1,0:T(8,128)(2,1)}) %all-gather.12.cloned.1.call-update) | async-done | bytes 4718608 | tf_op jit(solution)/shard_map/all_gather | solution.py:144
  256.1 3.8 fusion.123
  267.7 64.2 %all-gather.16.cloned.1.call-done = bf16[3072,768]{1,0:T(8,128)(2,1)} async-done(((bf16[384,768]{1,0:T(8,128)(2,1)}), bf16[3072,768]{1,0:T(8,128)(2,1)}) %all-gather.16.cloned.1.call-update) | async-done | bytes 4718608 | tf_op jit(solution)/shard_map/all_gather | solution.py:145
  332.0 4.5 fusion.122
  370.1 5.4 %fusion.42 = f32[384,8,96]{0,2,1:T(8,128)} fusion(bf16[512,8,96]{0,2,1:T(8,128)(2,1)S(1)} %bitcast.223, f32[384,8]{0,1:T(8,128)S(1)} %get-tuple-element.62, f32[384,8]{0,1:T(8,128)S(1)} %get-tuple-element.63, f32[8,384,512]{2,1,0:T(8,128)} %copy-done.4, f32[8,384]{1,0:T(8,128)S(1)} %get-tuple-element.64, pred[512]{0:T(512)(128)(4,1)S(1)} %get-tuple-element.88), kind=kOutput, calls=%fused_computation.104 | convolution fusion | flops 308871168 | bytes 8294912 | tf_op jit(solution)/shard_map/hqk,khe->hqe/dot_general | solution.py:163
  375.5 4.2 fusion.40
  379.7 3.1 fusion.38
  391.3 33.3 %all-gather.20.cloned.1.call-done = bf16[1536,3072]{1,0:T(8,128)(2,1)} async-done(((bf16[96,3072]{1,0:T(8,128)(2,1)}), bf16[1536,3072]{1,0:T(8,128)(2,1)}) %all-gather.20.cloned.1.call-update) | async-done | bytes 9437200 | tf_op jit(solution)/shard_map/all_gather | solution.py:129
  424.6 6.5 %fusion.45 = f32[384,3072]{1,0:T(8,128)S(1)} fusion(bf16[1536,3072]{1,0:T(8,128)(2,1)} %all-gather.20.cloned.1.call-done, bf16[384,1536]{1,0:T(8,128)(2,1)S(1)} %get-tuple-element.80, f32[384]{0:T(512)S(1)} %add_rsqrt_fusion, f32[384]{0:T(512)S(1)} %broadcast_multiply_fusion), kind=kOutput, calls=%fused_computation.110 | convolution fusion | flops 3626237952 | bytes 15338496 | tf_op jit(solution)/shard_map/dot_general | solution.py:178
  431.7 4.9 %collective-permute-start.1 = (bf16[15,1536]{1,0:T(8,128)(2,1)S(1)}, bf16[15,1536]{1,0:T(8,128)(2,1)S(1)}, u32[]{:S(2)}, u32[]{:S(2)}) collective-permute-start(bf16[15,1536]{1,0:T(8,128)(2,1)S(1)} %get-tuple-element.60), channel_id=1, source_target_pairs={{0,16},{16,32},{32,48},{48,64},{64,80},{80,96},{96,112},{1,17},{17... | collective-permute-start | bytes 138248 | tf_op jit(solution)/shard_map/ppermute | solution.py:27
  438.4 5.8 %collective-permute-done.2 = bf16[15,1536]{1,0:T(8,128)(2,1)S(1)} collective-permute-done((bf16[15,1536]{1,0:T(8,128)(2,1)S(1)}, bf16[15,1536]{1,0:T(8,128)(2,1)S(1)}, u32[]{:S(2)}, u32[]{:S(2)}) %collective-permute-start.2) | collective-permute-done | bytes 46112 | tf_op jit(solution)/shard_map/ppermute | solution.py:30
  444.1 12.1 %fusion.77 = bf16[1,384,1536]{2,1,0:T(8,128)(2,1)} fusion(f32[1536]{0:T(1024)S(1)} %get-tuple-element.34, bf16[15,1536]{1,0:T(8,128)(2,1)S(1)} %collective-permute-done.2, bf16[384,1536]{1,0:T(8,128)(2,1)S(1)} %fusion.31, f32[1536]{0:T(1024)S(1)} %get-tuple-element.35, f32[1536]{0:T(1024)S(1)} %get-tuple-element.6, f32[1536]{0:T(1024)S(1)} %get-tuple-element.7, ...), kind=kLoop, calls=%fused_computation.160 | loop fusion | flops 111476736 | bytes 3821568 | tf_op jit(solution)/shard_map/broadcast_in_dim | solution.py:187
  (127 shorter events, 72.1 us)
Async XLA Ops:
  6.5 145.5 %copy-start = (bf16[1152,128]{1,0:T(8,128)(2,1)S(1)}, bf16[1152,128]{1,0:T(8,128)(2,1)}, u32[]{:S(2)}) copy-start(bf16[1152,128]{1,0:T(8,128)(2,1)} %param.16) | copy-start | bytes 884740
  6.5 28.3 %copy-start.14 = (bf16[9,128]{1,0:T(8,128)(2,1)S(1)}, bf16[9,128]{1,0:T(8,128)(2,1)}, u32[]{:S(2)}) copy-start(bf16[9,128]{1,0:T(8,128)(2,1)} %param.15) | copy-start | bytes 6916
  6.5 171.6 %all-gather.10.cloned.1.call-start = ((), (), s32[]{:S(2)}) async-start(), calls=%async_computation.3 | async-start | bytes 2506752 | tf_op jit(solution)/shard_map/all_gather | solution.py:126
  7.3 174.7 %all-gather.14.cloned.1.call-start = ((), (), s32[]{:S(2)}) async-start(), calls=%async_computation.5 | async-start | bytes 2506752 | tf_op jit(solution)/shard_map/all_gather | solution.py:127
  9.4 20.5 %all-to-all-start = ((s32[128,1,12]{2,1,0:T(1,128)}), s32[128,1,12]{2,1,0:T(1,128)S(1)}, u32[]{:S(2)}, u32[]{:S(2)}) async-start(s32[128,1,12]{2,1,0:T(1,128)} %bitcast), calls=%async_computation | async-start | bytes 131072 | tf_op jit(solution)/shard_map/all_to_all | solution.py:107
  20.6 170.1 %all-gather.8.cloned.1.call-start = ((), (), s32[]{:S(2)}) async-start(), calls=%async_computation.2 | async-start | bytes 2506752 | tf_op jit(solution)/shard_map/all_gather | solution.py:125
  29.9 21.3 %all-to-all-start.1 = ((bf16[128,12,128]{2,1,0:T(8,128)(2,1)}), bf16[128,12,128]{2,1,0:T(8,128)(2,1)S(1)}, u32[]{:S(2)}, u32[]{:S(2)}) async-start(bf16[128,12,128]{2,1,0:T(8,128)(2,1)} %reshape.406), calls=%async_computation.1 | async-start | bytes 1048576 | tf_op jit(solution)/shard_map/all_to_all | solution.py:100
  34.8 221.3 %all-gather.12.cloned.1.call-start = ((), (), s32[]{:S(2)}) async-start(), calls=%async_computation.4 | async-start | bytes 5308416 | tf_op jit(solution)/shard_map/all_gather | solution.py:144
  55.9 11.2 %collective-permute-start = (bf16[3,128]{1,0:T(4,128)(2,1)S(1)}, bf16[3,128]{1,0:T(4,128)(2,1)S(1)}, u32[]{:S(2)}, u32[]{:S(2)}) collective-permute-start(bf16[3,128]{1,0:T(4,128)(2,1)S(1)} %slice.378), channel_id=1, source_target_pairs={{0,16},{16,32},{32,48},{48,64},{64,80},{80,96},{96,112},{1,17},{17... | collective-permute-start | bytes 2312 | tf_op jit(solution)/shard_map/ppermute | solution.py:19
  108.0 12.3 %copy-start.2 = (bf16[769,32,384]{2,1,0:T(8,128)(2,1)}, bf16[769,32,384]{2,1,0:T(8,128)(2,1)S(1)}, u32[]{:S(2)}) copy-start(bf16[769,32,384]{2,1,0:T(8,128)(2,1)S(1)} %fusion.7) | copy-start | bytes 56696836
  128.6 15.0 %slice-start = ((bf16[769,32,384]{2,1,0:T(8,128)(2,1)}), bf16[1,32,384]{2,1,0:T(8,128)(2,1)S(1)}, s32[]{:S(2)}) async-start(bf16[769,32,384]{2,1,0:T(8,128)(2,1)} %copy-done.2), calls=%async_computation.9 | async-start | bytes 49152 | tf_op jit(solution)/shard_map/slice | solution.py:68
  177.7 13.0 %copy-start.5 = (bf16[384,1536]{1,0:T(8,128)(2,1)}, bf16[384,1536]{1,0:T(8,128)(2,1)S(1)}, u32[]{:S(2)}) copy-start(bf16[384,1536]{1,0:T(8,128)(2,1)S(1)} %get-tuple-element.66) | copy-start | bytes 3538948
  181.8 5.1 %copy-start.15 = (s32[16]{0:T(128)S(1)}, s32[16]{0:T(128)}, u32[]{:S(2)}) copy-start(s32[16]{0:T(128)} %param.14) | copy-start | bytes 196
  181.8 8.5 %copy-start.13 = (bf16[31,1536]{1,0:T(8,128)(2,1)S(1)}, bf16[31,1536]{1,0:T(8,128)(2,1)}, u32[]{:S(2)}) copy-start(bf16[31,1536]{1,0:T(8,128)(2,1)} %param.23) | copy-start | bytes 285700
  181.9 150.1 %all-gather.16.cloned.1.call-start = ((), (), s32[]{:S(2)}) async-start(), calls=%async_computation.6 | async-start | bytes 5308416 | tf_op jit(solution)/shard_map/all_gather | solution.py:145
  185.6 202.3 %all-gather.18.cloned.1.call-start = ((), (), s32[]{:S(2)}) async-start(), calls=%async_computation.7 | async-start | bytes 2506752 | tf_op jit(solution)/shard_map/all_gather | solution.py:128
  186.1 238.5 %all-gather.20.cloned.1.call-start = ((), (), s32[]{:S(2)}) async-start(), calls=%async_computation.8 | async-start | bytes 10027008 | tf_op jit(solution)/shard_map/all_gather | solution.py:129
  350.4 2.4 copy-start.8
  352.8 6.9 %copy-start.4 = (f32[8,384,512]{2,1,0:T(8,128)}, f32[8,384,512]{2,1,0:T(8,128)S(1)}, u32[]{:S(2)}) copy-start(f32[8,384,512]{2,1,0:T(8,128)S(1)} %get-tuple-element.78) | copy-start | bytes 18874372
  352.9 1.7 copy-start.7
  354.1 7.3 %copy-start.3 = (f32[8,384,512]{2,1,0:T(8,128)}, f32[8,384,512]{2,1,0:T(8,128)S(1)}, u32[]{:S(2)}) copy-start(f32[8,384,512]{2,1,0:T(8,128)S(1)} %get-tuple-element.76) | copy-start | bytes 18874372
  368.3 1.8 copy-start.12
  368.3 7.2 %slice-start.1 = ((s8[6291456]{0:T(1024)(128)(4,1)}), s8[4194304]{0:T(1024)(128)(4,1)S(1)}, s32[]{:S(2)}) async-start(s8[6291456]{0:T(1024)(128)(4,1)} %bitcast.205), calls=%async_computation.10 | async-start | bytes 8388608
  370.1 5.4 %slice-start.2 = ((s8[6291456]{0:T(1024)(128)(4,1)}), s8[2097152]{0:T(1024)(128)(4,1)S(1)}, s32[]{:S(2)}) async-start(s8[6291456]{0:T(1024)(128)(4,1)} %bitcast.205), calls=%async_computation.11 | async-start | bytes 4194304
  379.7 3.1 copy-start.11
  382.8 1.5 copy-start.10
  384.3 1.5 copy-start.9
  385.8 2.1 copy-start.6
  431.1 25.2 %copy-start.1 = (bf16[1152,128]{1,0:T(8,128)(2,1)S(1)}, bf16[1152,128]{1,0:T(8,128)(2,1)}, u32[]{:S(2)}) copy-start(bf16[1152,128]{1,0:T(8,128)(2,1)} %param.16) | copy-start | bytes 884740
  431.7 6.6 %collective-permute-start.1 = (bf16[15,1536]{1,0:T(8,128)(2,1)S(1)}, bf16[15,1536]{1,0:T(8,128)(2,1)S(1)}, u32[]{:S(2)}, u32[]{:S(2)}) collective-permute-start(bf16[15,1536]{1,0:T(8,128)(2,1)S(1)} %get-tuple-element.60), channel_id=1, source_target_pairs={{0,16},{16,32},{32,48},{48,64},{64,80},{80,96},{96,112},{1,17},{17... | collective-permute-start | bytes 138248 | tf_op jit(solution)/shard_map/ppermute | solution.py:27
  436.6 7.5 %collective-permute-start.2 = (bf16[15,1536]{1,0:T(8,128)(2,1)S(1)}, bf16[15,1536]{1,0:T(8,128)(2,1)S(1)}, u32[]{:S(2)}, u32[]{:S(2)}) collective-permute-start(bf16[15,1536]{1,0:T(8,128)(2,1)S(1)} %get-tuple-element.61), channel_id=1, source_target_pairs={{16,0},{32,16},{48,32},{64,48},{80,64},{96,80},{112,96},{17,1},{33... | collective-permute-start | bytes 138248 | tf_op jit(solution)/shard_map/ppermute | solution.py:30
Sparse Core Ops, SparseCore 0:
  9.1 40.2 all-gather.9
  51.0 35.6 all-gather.13
  88.5 34.4 all-gather.7
  181.9 74.0 all-gather.11
  258.2 73.6 all-gather.15
  333.5 32.0 all-gather.17
  367.3 57.2 all-gather.19
where the time goes:
time: 473 us; the launch traced here: 464 us
  waiting for transfers between devices  190 us (40%)
  local copies, waits for them, and re-layouts  101 us (21%)
  matrix products  85.9 us (18%)
  other arithmetic  46.9 us (10%)
  starting transfers between devices  24.7 us (5%)
  between operations  14.5 us (3%)
    all_gather x1, waiting for transfers between devices, local(): value_part = lax.all_gather(values, 'ctx', axis=0, tiled=True)  64.2 us
    all_gather x1, waiting for transfers between devices, local(): key_part = lax.all_gather(key_rows, 'ctx', axis=0, tiled=True)  62.1 us
    all_gather x1, waiting for transfers between devices, local(): lax.all_gather(pw1, 'sess', axis=0, tiled=True)  33.3 us
    slice x7, local copies, waits for them, and re-layouts, local(): value_part[offset:offset + block_rows].reshape(block_rows, HEADS, HEAD)  18.4 us
    dot_general x6, matrix products, local(): jnp.einsum('hqk,khe->hqe', weights, value_block, preferred_element_type=j...  17.7 us
    dot_general x1, matrix products, first_conv(): running = jnp.dot(patches, banded, preferred_element_type=jnp.float32)  15.3 us
    slice x1, local copies, waits for them, and re-layouts, second_conv(): row_pairs[:, 0]  15 us
    all_to_all x1, waiting for transfers between devices, local(): lax.all_to_all(mel_in.reshape(rank_count, slot_rows, mel_width), ('ctx',...  14.6 us
  transfers between devices with their start and end apart: 12, of which 7 were waited for; matrix products, arithmetic and copies ran while one was open for 46% of the time, Pallas kernels for 0%

commit v1 on v0

v1 whole, which is shorter than its diff:
```python
import functools
import math

import jax
import jax.numpy as jnp
from jax import lax
from jax.experimental import pallas as pl
from jax.experimental.pallas import tpu as pltpu
from jax.sharding import PartitionSpec as P

HEADS = 8
HEAD = 96
KERNEL = 31
EPS = 1e-05
ROWS = 384
PAD = 16
SLOT = 12
RANKS = 128
D = 1536
F32 = jnp.float32
BF16 = jnp.bfloat16
VMEM = pltpu.VMEM
MIB = 1024 * 1024


def vspec():
    return pl.BlockSpec(memory_space=pltpu.VMEM)


def dot(a, b):
    return jnp.dot(a, b, preferred_element_type=F32)


def iota(shape, dim):
    return lax.broadcasted_iota(jnp.int32, shape, dim)


def layer_norm(values):
    row_mean = jnp.mean(values, axis=-1, keepdims=True)
    centred = values - row_mean
    variance = jnp.mean(centred * centred, axis=-1, keepdims=True)
    return (centred * lax.rsqrt(variance + EPS)).astype(BF16)


def place_kernel(arrived, out, wide, sorted_rows):
    wide[...] = arrived[...].astype(F32)
    high = wide[pl.ds(SLOT, RANKS, stride=16), :]
    low = wide[pl.ds(SLOT + 1, RANKS, stride=16), :]
    position = (high * 64.0 + low).T
    for r in range(SLOT):
        sorted_rows[r * RANKS : (r + 1) * RANKS, :] = wide[pl.ds(r, RANKS, stride=16), :].astype(BF16)
    target = iota((ROWS, RANKS), 0).astype(F32) * 4.0
    for k in range(4):
        chosen = jnp.concatenate(
            [
                jnp.where(position[r : r + 1, :] == target + float(k), 1.0, 0.0).astype(BF16)
                for r in range(SLOT)
            ],
            axis=1,
        )
        out[:, 128 * k : 128 * (k + 1)] = dot(chosen, sorted_rows[...]).astype(BF16)


def place(arrived):
    return pl.pallas_call(
        place_kernel,
        out_shape=jax.ShapeDtypeStruct((ROWS, 512), BF16),
        in_specs=[vspec()],
        out_specs=vspec(),
        scratch_shapes=[VMEM((16 * RANKS, 128), F32), VMEM((SLOT * RANKS, 128), BF16)],
        compiler_params=pltpu.CompilerParams(vmem_limit_bytes=24 * MIB),
        name="place_frames",
    )(arrived)


def conv_kernel(
    x, halo, first, second, lin_hbm,
    emb_out, norm_out,
    lin, last, sel, win_e, win_o, band, taps, even, odd, behind, sub, sem,
):
    copy = pltpu.make_async_copy(lin_hbm, lin, sem)
    copy.start()
    total = ROWS + PAD
    row = iota((384, 512), 0)
    col = iota((384, 512), 1)
    a = row // 128
    m = row % 128
    p = col // 32
    r = col % 32
    a2 = jnp.where(r >= 9, 1, 0) + jnp.where(r >= 18, 1, 0)
    i = r - 9 * a2
    hit = (r < 27) & (a == a2) & (m == 8 * p - 1 + i)
    sel[...] = jnp.where(hit, 1.0, 0.0).astype(BF16)
    brow = iota((128, 128), 0)
    kern = first[...].astype(F32)
    for f in range(16):
        block = jnp.zeros((128, 128), F32)
        for tap in range(9):
            at = 32 * (f // 4) + 9 * (tap // 3) + 2 * (f % 4) + tap % 3
            block = jnp.where(brow == at, kern[tap : tap + 1, :], block)
        band[:, 128 * f : 128 * (f + 1)] = block.astype(BF16)
    taps[...] = jnp.zeros_like(taps)
    for place_of, row_tap in enumerate((1, 2, 0)):
        for o in range(2):
            for b in range(3):
                at = 640 * place_of + 128 * (2 * o + b)
                source = (3 * row_tap + b) * 128
                taps[at : at + 128, 128 * o : 128 * (o + 1)] = second[source : source + 128, :]

    last[0:PAD, :] = halo[:, 384:512].astype(F32)
    last[PAD:total, :] = x[:, 384:512].astype(F32)
    previous = last[pl.ds(PAD - 1, ROWS), :].astype(BF16)
    win_e[...] = dot(jnp.concatenate([previous, x[:, 0:256]], axis=1), sel[...]).astype(BF16)
    win_o[0:PAD, :] = dot(halo[:, 128:512], sel[...]).astype(BF16)
    win_o[PAD:total, :] = dot(x[:, 128:512], sel[...]).astype(BF16)
    even[:, 0:128] = jnp.zeros((ROWS, 128), BF16)
    odd[:, 0:128] = jnp.zeros((total, 128), BF16)

    def group(g, carry):
        q = pl.multiple_of((g // 4) * 128, 128)
        bcol = pl.multiple_of((g % 4) * 512, 512)
        to = pl.multiple_of(128 + g * 512, 128)
        weights = band[:, pl.ds(bcol, 512)]
        even[:, pl.ds(to, 512)] = jnp.maximum(dot(win_e[:, pl.ds(q, 128)], weights), 0.0).astype(BF16)
        odd[:, pl.ds(to, 512)] = jnp.maximum(dot(win_o[:, pl.ds(q, 128)], weights), 0.0).astype(BF16)
        at = pl.multiple_of(g * 512, 512)
        odd_part = odd[:, pl.ds(at, 640)]
        behind[...] = dot(odd_part, taps[1280:1920, :])
        both = jnp.concatenate([even[:, pl.ds(at, 640)], odd[PAD:total, pl.ds(at, 640)]], axis=1)
        here = dot(both, taps[0:1280, :]) + behind[pl.ds(PAD - 1, ROWS), :]
        sub[:, pl.ds(pl.multiple_of(g * 256, 256), 256)] = jnp.maximum(here, 0.0).astype(BF16)
        return carry

    lax.fori_loop(0, 16, group, 0)
    copy.wait()

    def project(n, carry):
        at = pl.multiple_of(n * 512, 512)
        emb_out[:, pl.ds(at, 512)] = dot(sub[...], lin[:, pl.ds(at, 512)]).astype(BF16)
        return carry

    lax.fori_loop(0, 3, project, 0)
    norm_out[...] = layer_norm(emb_out[...].astype(F32))


def convolve(x, halo, first, second, lin_in):
    total = ROWS + PAD
    return pl.pallas_call(
        conv_kernel,
        out_shape=[jax.ShapeDtypeStruct((ROWS, D), BF16)] * 2,
        in_specs=[vspec()] * 4 + [pl.BlockSpec(memory_space=pl.ANY)],
        out_specs=[vspec()] * 2,
        scratch_shapes=[
            VMEM((4096, D), BF16),
            VMEM((total, 128), F32),
            VMEM((384, 512), BF16),
            VMEM((ROWS, 512), BF16),
            VMEM((total, 512), BF16),
            VMEM((128, 2048), BF16),
            VMEM((1920, 256), BF16),
            VMEM((ROWS, 8320), BF16),
            VMEM((total, 8320), BF16),
            VMEM((total, 256), F32),
            VMEM((ROWS, 4096), BF16),
            pltpu.SemaphoreType.DMA,
        ],
        compiler_params=pltpu.CompilerParams(vmem_limit_bytes=52 * MIB),
        cost_estimate=pl.CostEstimate(flops=14_000_000_000, bytes_accessed=14_000_000, transcendentals=0),
        name="subsample",
    )(x, halo, first, second, lin_in)


def qkv_kernel(live_rows, normed, weights, out):
    lane = iota((ROWS, 128), 1)
    live = iota((ROWS, 128), 0) < live_rows[0]
    for part in range(3):
        rows = dot(normed[...], weights[:, 768 * part : 768 * (part + 1)])
        if part == 1:
            extra = jnp.where(live, 0.0, -1e30)
        else:
            extra = jnp.ones((ROWS, 128), F32)
        for h in range(HEADS):
            base, shift = (96 * h) // 128 * 128, (96 * h) % 128
            if shift == 0:
                head = rows[:, base : base + 128]
            elif shift == 32:
                head = pltpu.roll(rows[:, base : base + 128], 128 - shift, 1)
            else:
                head = pltpu.roll(rows[:, base : base + 256], 256 - shift, 1)[:, 0:128]
            head = jnp.where(lane < HEAD, head, jnp.where(lane == HEAD, extra, 0.0))
            out[h, :, 128 * part : 128 * (part + 1)] = head.astype(BF16)


def qkv(live_rows, normed, weights):
    return pl.pallas_call(
        qkv_kernel,
        out_shape=jax.ShapeDtypeStruct((HEADS, ROWS, 384), BF16),
        in_specs=[pl.BlockSpec(memory_space=pltpu.SMEM), vspec(), vspec()],
        out_specs=vspec(),
        compiler_params=pltpu.CompilerParams(vmem_limit_bytes=40 * MIB),
        cost_estimate=pl.CostEstimate(flops=2_700_000_000, bytes_accessed=10_000_000, transcendentals=0),
        name="project_heads",
    )(live_rows, normed, weights)


QBLOCK = 256


def attend_kernel(queries, rows, out):
    keys = rows[:, 128:256]
    scores = lax.dot_general(
        queries[:, 0:128], keys, (((1,), (1,)), ((), ())), preferred_element_type=F32
    )
    scale = math.log2(math.e) / math.sqrt(HEAD)
    row_max = jnp.max(scores, axis=1, keepdims=True)
    weights = jnp.exp2((scores - row_max) * scale).astype(BF16)
    total = dot(weights, rows[:, 256:384])
    lane = iota(total.shape, 1)
    result = total / total[:, HEAD : HEAD + 1]
    out[...] = jnp.where(lane < HEAD, result, 0.0).astype(BF16)


def attend(rows):
    count = rows.shape[0]
    return pl.pallas_call(
        attend_kernel,
        grid=(count // QBLOCK,),
        out_shape=jax.ShapeDtypeStruct((count, 128), BF16),
        in_specs=[
            pl.BlockSpec((QBLOCK, 384), lambda i: (i, 0)),
            vspec(),
        ],
        out_specs=pl.BlockSpec((QBLOCK, 128), lambda i: (i, 0)),
        compiler_params=pltpu.CompilerParams(vmem_limit_bytes=40 * MIB),
        cost_estimate=pl.CostEstimate(flops=5_000_000_000, bytes_accessed=4_000_000, transcendentals=9_400_000),
        name="attend_head",
    )(rows, rows)


def gate_kernel(live_rows, heads, emb, gathered, residual_out, gated_out, w_out):
    for s in range(16):
        for half in range(2):
            block = gathered[96 * s + 48 * half : 96 * s + 48 * (half + 1), 3072:3840]
            w_out[48 * s : 48 * (s + 1), 768 * half : 768 * (half + 1)] = block
    w_out[768:800, :] = jnp.zeros((32, D), BF16)
    total = emb[...].astype(F32)
    for pair in range(4):
        left = jnp.concatenate([heads[2 * pair], heads[2 * pair + 1]], axis=1)
        at = 192 * pair
        right = jnp.concatenate([w_out[at : at + 128, :], w_out[at + 96 : at + 224, :]], axis=0)
        total = total + dot(left, right)
    residual = total.astype(BF16)
    residual_out[...] = residual
    normed = layer_norm(residual.astype(F32))
    live = iota((ROWS, 256), 0) < live_rows[0]
    for n in range(6):
        value = dot(normed, gathered[:, 256 * n : 256 * (n + 1)])
        gate = dot(normed, gathered[:, D + 256 * n : D + 256 * (n + 1)])
        gated = jnp.where(live, value * jax.nn.sigmoid(gate), 0.0)
        gated_out[:, 256 * n : 256 * (n + 1)] = gated.astype(BF16)


def gate(live_rows, heads, emb, gathered):
    return pl.pallas_call(
        gate_kernel,
        out_shape=[jax.ShapeDtypeStruct((ROWS, D), BF16)] * 2,
        in_specs=[pl.BlockSpec(memory_space=pltpu.SMEM), vspec(), vspec(), vspec()],
        out_specs=[vspec()] * 2,
        scratch_shapes=[VMEM((800, D), BF16)],
        compiler_params=pltpu.CompilerParams(vmem_limit_bytes=48 * MIB),
        cost_estimate=pl.CostEstimate(flops=4_600_000_000, bytes_accessed=15_000_000, transcendentals=600_000),
        name="gate_rows",
    )(live_rows, heads, emb, gathered)


def depth_kernel(low, gated, high, residual, kernel, out, wide):
    wide[0:PAD, :] = low[...].astype(F32)
    wide[PAD : PAD + ROWS, :] = gated[...].astype(F32)
    wide[PAD + ROWS :, :] = high[...].astype(F32)
    weights = kernel[...].astype(F32)
    chunk = 64
    for start in range(0, ROWS, chunk):
        total = jnp.zeros((chunk, 128), F32)
        for j in range(KERNEL):
            total = total + wide[pl.ds(start + j + 1, chunk), :] * weights[j : j + 1, :]
        rows = residual[start : start + chunk, :].astype(F32) + total * jax.nn.sigmoid(total)
        out[start : start + chunk, :] = rows.astype(BF16)


def depthwise(low, gated, high, residual, kernel):
    column = lambda rows: pl.BlockSpec((rows, 128), lambda n: (0, n))
    return pl.pallas_call(
        depth_kernel,
        grid=(D // 128,),
        out_shape=jax.ShapeDtypeStruct((ROWS, D), BF16),
        in_specs=[column(PAD), column(ROWS), column(PAD), column(ROWS), column(32)],
        out_specs=column(ROWS),
        scratch_shapes=[VMEM((ROWS + 2 * PAD, 128), F32)],
        compiler_params=pltpu.CompilerParams(vmem_limit_bytes=24 * MIB),
        name="depthwise",
    )(low, gated, high, residual, kernel)


def shifted(block, axis, step):
    count = lax.axis_size(axis)
    route = [(i, i + step) for i in range(count) if 0 <= i + step < count]
    return lax.ppermute(block, axis, route)


def local(mel_in, route, lengths, conv_first, conv_second, lin_in, wq, wk, wv, wo, pw1, dw_kernel):
    w_qkv = lax.all_gather(jnp.concatenate([wq, wk, wv], axis=1), "sess", axis=0, tiled=True)
    tail = jnp.concatenate([pw1, jnp.concatenate([wo[:, :768], wo[:, 768:]], axis=0)], axis=1)
    w_tail = lax.all_gather(tail, "sess", axis=0, tiled=True)

    position = jnp.pad(route.reshape(RANKS, 1, SLOT), ((0, 0), (0, 0), (0, 128 - SLOT)))
    slots = jnp.concatenate(
        [
            mel_in.reshape(RANKS, SLOT, 128),
            (position // 64).astype(BF16),
            (position % 64).astype(BF16),
            jnp.zeros((RANKS, 2, 128), BF16),
        ],
        axis=1,
    )
    arrived = lax.all_to_all(slots, ("ctx", "sess"), split_axis=0, concat_axis=0, tiled=True)
    frames = place(arrived.reshape(16 * RANKS, 128))
    halo = shifted(frames[ROWS - PAD :], "ctx", 1)
    first = jnp.pad(conv_first, ((0, 7), (0, 0)))
    embedded, normed = convolve(frames, halo, first, conv_second, lin_in)

    length = lengths[lax.axis_index("sess")]
    live_rows = (length - lax.axis_index("ctx") * ROWS).reshape(1)
    sent = qkv(live_rows, normed, w_qkv)
    held = lax.all_to_all(sent, "ctx", split_axis=0, concat_axis=0, tiled=True)
    context = attend(held.reshape(HEADS * ROWS, 384))
    heads = lax.all_to_all(context.reshape(HEADS, ROWS, 128), "ctx", split_axis=0, concat_axis=0, tiled=True)
    residual, gated = gate(live_rows, heads, embedded, w_tail)
    low = shifted(gated[ROWS - PAD :], "ctx", 1)
    high = shifted(gated[:PAD], "ctx", -1)
    encoded = depthwise(low, gated, high, residual, jnp.pad(dw_kernel, ((0, 1), (0, 0))))
    return encoded[None]


def solution(mesh):
    return jax.shard_map(
        local,
        mesh=mesh,
        in_specs=(
            P(("ctx", "sess"), None),
            P(("ctx", "sess")),
            P(),
            P(),
            P(),
            P(),
            P("sess", None),
            P("sess", None),
            P("sess", None),
            P("sess", None),
            P("sess", None),
            P(),
        ),
        out_specs=P("sess", "ctx", None),
        check_vma=False,
    )
```

time: 473 us -> 205 us (0.43)
  the two profiles are of different devices: /device:TPU:0 before, /device:TPU:1 now
where the time goes in v1:
time: 205 us; the launch traced here: 204 us
  blocking collectives  88.8 us (43%)
  Pallas kernels  59.5 us (29%)
  waiting for transfers between devices  23.2 us (11%)
  between operations  14.3 us (7%)
  starting transfers between devices  8.3 us (4%)
  local copies, waits for them, and re-layouts  6.18 us (3%)
  other arithmetic  3.77 us (2%)
    all_to_all x1, blocking collectives, local(): held = lax.all_to_all(sent, 'ctx', split_axis=0, concat_axis=0, tiled=True)  40.3 us
    all_to_all x1, blocking collectives, local(): lax.all_to_all(slots, ('ctx', 'sess'), split_axis=0, concat_axis=0, tiled...  30.6 us
    pallas_call x1, Pallas kernels, convolve(): pl.pallas_call(conv_kernel, out_shape=[jax.ShapeDtypeStruct((ROWS, D), BF...  22.5 us
    all_gather x1, waiting for transfers between devices, local(): w_tail = lax.all_gather(tail, 'sess', axis=0, tiled=True)  18.1 us
    all_to_all x1, blocking collectives, local(): lax.all_to_all(context.reshape(HEADS, ROWS, 128), 'ctx', split_axis=0, co...  17.9 us
    pallas_call x1, Pallas kernels, attend(): pl.pallas_call(attend_kernel, grid=(count // QBLOCK,), out_shape=jax.Shap...  15 us
    pallas_call x1, Pallas kernels, gate(): pl.pallas_call(gate_kernel, out_shape=[jax.ShapeDtypeStruct((ROWS, D), BF...  10.1 us
    ppermute x3, starting transfers between devices, shifted(): return lax.ppermute(block, axis, route)  8.25 us
  transfers between devices with their start and end apart: 5, of which 2 were waited for; matrix products, arithmetic and copies ran while one was open for 2% of the time, Pallas kernels for 21%

profile of v1, /device:TPU:1, one launch (start us, length us, event | category | flops | bytes accessed | tf_op | source)
XLA Modules:
  0.0 204.0 jit_solution(7471368807890068076)
XLA Ops:
  6.5 1.9 pad_maximum_fusion
  8.4 0.0 all-gather.3.cloned.1.call-update
  8.5 0.0 all-gather.5.cloned.1.call-start
  8.5 1.0 fusion.3
  9.5 0.9 maximum_maximum_fusion
  10.4 0.0 all-gather.5.cloned.1.call-update
  10.5 0.1 reshape.20
  10.6 0.1 reshape.19
  10.7 0.1 pad.24.clone
  10.8 0.3 fusion.1
  11.1 0.1 fusion
  11.3 0.0 copy-start.8
  11.3 0.0 copy-start.2
  11.3 0.5 maximum_maximum_fusion.1
  11.8 30.6 %all_to_all.15 = bf16[128,16,128]{2,1,0:T(8,128)(2,1)S(1)} all-to-all(bf16[128,16,128]{2,1,0:T(8,128)(2,1)S(1)} %maximum_maximum_fusion.1), channel_id=1, replica_groups=mesh['ctx'=8,'sess'=16] {'ctx','sess'}, dimensions={0} | all-to-all | bytes 1048576 | tf_op jit(solution)/shard_map/all_to_all | solution.py:325
  42.4 1.6 place_frames.1.x
  43.9 2.5 %collective-permute-start = (bf16[16,512]{1,0:T(8,128)(2,1)S(1)}, bf16[16,512]{1,0:T(8,128)(2,1)S(1)}, u32[]{:S(2)}, u32[]{:S(2)}) collective-permute-start(bf16[16,512]{1,0:T(8,128)(2,1)S(1)} %slice.20), channel_id=1, source_target_pairs={{0,16},{16,32},{32,48},{48,64},{64,80},{80,96},{96,112},{1,17},{17... | collective-permute-start | bytes 49160 | tf_op jit(solution)/shard_map/ppermute | solution.py:307
  46.5 0.6 dynamic_slice.3
  47.7 22.5 %subsample.1 = (bf16[384,1536]{1,0:T(8,128)(2,1)S(1)}, bf16[384,1536]{1,0:T(8,128)(2,1)}) custom-call(bf16[384,512]{1,0:T(8,128)(2,1)S(1)} %place_frames.1.x, bf16[16,512]{1,0:T(8,128)(2,1)S(1)} %collective-permute-done.halo, bf16[16,128]{1,0:T(8,128)(2,1)S(1)} %pad.13.first, bf16[1152,128]{1,0:T(8,128)(2,1)S(1)} %copy-done.2, bf16[4096,1536]{1,0:T(8,128)(2,1)} %lin_hbm.1), custom_call_target="tpu_custom_call" | custom-call | flops 14000000000 | bytes 14000000 | tf_op jit(solution)/shard_map/subsample/pallas_call | solution.py:148
  70.3 0.0 all-gather.3.cloned.1.call-done.weights
  70.3 3.0 %copy-done = bf16[1536,2304]{1,0:T(8,128)(2,1)S(1)} copy-done((bf16[1536,2304]{1,0:T(8,128)(2,1)S(1)}, bf16[1536,2304]{1,0:T(8,128)(2,1)}, u32[]{:S(2)}) %copy-start) | copy-done | bytes 7077912
  73.3 1.3 copy-done.1
  74.6 3.1 %project_heads.1 = bf16[8,384,384]{2,1,0:T(8,128)(2,1)S(1)} custom-call(s32[1]{0:T(128)} %bitcast.1.live_rows, bf16[384,1536]{1,0:T(8,128)(2,1)S(1)} %copy-done.1, bf16[1536,2304]{1,0:T(8,128)(2,1)S(1)} %copy-done), custom_call_target="tpu_custom_call" | custom-call | flops 2700000000 | bytes 10000000 | tf_op jit(solution)/shard_map/project_heads/pallas_call | solution.py:195
  77.6 40.3 %all_to_all.16 = bf16[8,384,384]{2,1,0:T(8,128)(2,1)S(1)} all-to-all(bf16[8,384,384]{2,1,0:T(8,128)(2,1)S(1)} %project_heads.1), channel_id=1, replica_groups=mesh['ctx'=8,'sess'=16] {'ctx'}, dimensions={0} | all-to-all | bytes 4718592 | tf_op jit(solution)/shard_map/all_to_all | solution.py:334
  117.9 15.0 %attend_head.1 = bf16[3072,128]{1,0:T(8,128)(2,1)S(1)} custom-call(bf16[3072,384]{1,0:T(8,128)(2,1)S(1)} %bitcast.7, bf16[3072,384]{1,0:T(8,128)(2,1)S(1)} %bitcast.8), custom_call_target="tpu_custom_call" | custom-call | flops 5000000000 | bytes 4000000 | tf_op jit(solution)/shard_map/attend_head/pallas_call | solution.py:225
  133.0 17.9 %all_to_all.17.heads = bf16[8,384,128]{2,1,0:T(8,128)(2,1)S(1)} all-to-all(bf16[8,384,128]{2,1,0:T(8,128)(2,1)S(1)} %bitcast.10), channel_id=1, replica_groups=mesh['ctx'=8,'sess'=16] {'ctx'}, dimensions={0} | all-to-all | bytes 1572864 | tf_op jit(solution)/shard_map/all_to_all | solution.py:336
  150.9 18.1 %all-gather.5.cloned.1.call-done.gathered = bf16[1536,3840]{1,0:T(8,128)(2,1)} async-done(((bf16[96,3840]{1,0:T(8,128)(2,1)}), bf16[1536,3840]{1,0:T(8,128)(2,1)}) %all-gather.5.cloned.1.call-update) | async-done | bytes 11796496 | tf_op jit(solution)/shard_map/all_gather | solution.py:313
  169.0 10.1 %gate_rows.1 = (bf16[384,1536]{1,0:T(8,128)(2,1)S(1)}, bf16[384,1536]{1,0:T(8,128)(2,1)S(1)}) custom-call(s32[1]{0:T(128)} %bitcast.1.live_rows, bf16[8,384,128]{2,1,0:T(8,128)(2,1)S(1)} %all_to_all.17.heads, bf16[384,1536]{1,0:T(8,128)(2,1)S(1)} %get-tuple-element.10.emb, bf16[1536,3840]{1,0:T(8,128)(2,1)} %all-gather.5.cloned.1.call-done.gathered), custom_call_target="tpu_custom_call" | custom-call | flops 4600000000 | bytes 15000000 | tf_op jit(solution)/shard_map/gate_rows/pallas_call | solution.py:264
  179.1 4.5 %collective-permute-start.1 = (bf16[16,1536]{1,0:T(8,128)(2,1)S(1)}, bf16[16,1536]{1,0:T(8,128)(2,1)S(1)}, u32[]{:S(2)}, u32[]{:S(2)}) collective-permute-start(bf16[16,1536]{1,0:T(8,128)(2,1)S(1)} %get-tuple-element.16), channel_id=1, source_target_pairs={{0,16},{16,32},{32,48},{48,64},{64,80},{80,96},{96,112},{1,17},{17... | collective-permute-start | bytes 147464 | tf_op jit(solution)/shard_map/ppermute | solution.py:307
  183.5 1.3 collective-permute-start.2
  184.9 5.0 %collective-permute-done.2.high = bf16[16,1536]{1,0:T(8,128)(2,1)S(1)} collective-permute-done((bf16[16,1536]{1,0:T(8,128)(2,1)S(1)}, bf16[16,1536]{1,0:T(8,128)(2,1)S(1)}, u32[]{:S(2)}, u32[]{:S(2)}) %collective-permute-start.2) | collective-permute-done | bytes 49184 | tf_op jit(solution)/shard_map/ppermute | solution.py:307
  189.9 7.3 %depthwise.1 = bf16[384,1536]{1,0:T(8,128)(2,1)} custom-call(bf16[16,1536]{1,0:T(8,128)(2,1)S(1)} %collective-permute-done.1.low, bf16[384,1536]{1,0:T(8,128)(2,1)S(1)} %get-tuple-element.11.gated, bf16[16,1536]{1,0:T(8,128)(2,1)S(1)} %collective-permute-done.2.high, bf16[384,1536]{1,0:T(8,128)(2,1)S(1)} %get-tuple-element.12.residual, ...), custom_call_target="tpu_custom_call" | custom-call | tf_op jit(solution)/shard_map/depthwise/pallas_call | solution.py:292
  (22 shorter events, 0.1 us)
Async XLA Ops:
  6.5 3.0 %copy-start.3 = (bf16[96,3072]{1,0:T(8,128)(2,1)S(1)}, bf16[96,3072]{1,0:T(8,128)(2,1)}, u32[]{:S(2)}) copy-start(bf16[96,3072]{1,0:T(8,128)(2,1)} %param.22) | copy-start | bytes 1769476
  6.5 63.7 %all-gather.3.cloned.1.call-start = ((), (), s32[]{:S(2)}) async-start(), calls=%async_computation.3 | async-start | bytes 7520256 | tf_op jit(solution)/shard_map/all_gather | solution.py:311
  8.4 2.0 copy-start.6
  8.4 2.2 %copy-start.4 = (bf16[1536,128]{1,0:T(8,128)(2,1)S(1)}, bf16[1536,128]{1,0:T(8,128)(2,1)}, u32[]{:S(2)}) copy-start(bf16[1536,128]{1,0:T(8,128)(2,1)} %param.12) | copy-start | bytes 1179652
  8.5 160.5 %all-gather.5.cloned.1.call-start = ((), (), s32[]{:S(2)}) async-start(), calls=%async_computation.4 | async-start | bytes 12533760 | tf_op jit(solution)/shard_map/all_gather | solution.py:313
  11.3 35.2 %copy-start.7 = (bf16[9,128]{1,0:T(8,128)(2,1)S(1)}, bf16[9,128]{1,0:T(8,128)(2,1)}, u32[]{:S(2)}) copy-start(bf16[9,128]{1,0:T(8,128)(2,1)} %param.15) | copy-start | bytes 6916
  11.3 35.2 %copy-start.8 = (s32[16]{0:T(128)S(1)}, s32[16]{0:T(128)}, u32[]{:S(2)}) copy-start(s32[16]{0:T(128)} %param.14) | copy-start | bytes 196
  11.3 36.5 %copy-start.2 = (bf16[1152,128]{1,0:T(8,128)(2,1)S(1)}, bf16[1152,128]{1,0:T(8,128)(2,1)}, u32[]{:S(2)}) copy-start(bf16[1152,128]{1,0:T(8,128)(2,1)} %second.1) | copy-start | bytes 884740
  43.9 3.8 %collective-permute-start = (bf16[16,512]{1,0:T(8,128)(2,1)S(1)}, bf16[16,512]{1,0:T(8,128)(2,1)S(1)}, u32[]{:S(2)}, u32[]{:S(2)}) collective-permute-start(bf16[16,512]{1,0:T(8,128)(2,1)S(1)} %slice.20), channel_id=1, source_target_pairs={{0,16},{16,32},{32,48},{48,64},{64,80},{80,96},{96,112},{1,17},{17... | collective-permute-start | bytes 49160 | tf_op jit(solution)/shard_map/ppermute | solution.py:307
  70.3 3.0 %copy-start = (bf16[1536,2304]{1,0:T(8,128)(2,1)S(1)}, bf16[1536,2304]{1,0:T(8,128)(2,1)}, u32[]{:S(2)}) copy-start(bf16[1536,2304]{1,0:T(8,128)(2,1)} %all-gather.3.cloned.1.call-done.weights) | copy-start | bytes 21233668
  73.3 1.3 copy-start.1
  169.0 15.9 %copy-start.5 = (bf16[31,1536]{1,0:T(8,128)(2,1)S(1)}, bf16[31,1536]{1,0:T(8,128)(2,1)}, u32[]{:S(2)}) copy-start(bf16[31,1536]{1,0:T(8,128)(2,1)} %param.23) | copy-start | bytes 285700
  179.1 5.8 %collective-permute-start.1 = (bf16[16,1536]{1,0:T(8,128)(2,1)S(1)}, bf16[16,1536]{1,0:T(8,128)(2,1)S(1)}, u32[]{:S(2)}, u32[]{:S(2)}) collective-permute-start(bf16[16,1536]{1,0:T(8,128)(2,1)S(1)} %get-tuple-element.16), channel_id=1, source_target_pairs={{0,16},{16,32},{32,48},{48,64},{64,80},{80,96},{96,112},{1,17},{17... | collective-permute-start | bytes 147464 | tf_op jit(solution)/shard_map/ppermute | solution.py:307
  183.5 6.3 %collective-permute-start.2 = (bf16[16,1536]{1,0:T(8,128)(2,1)S(1)}, bf16[16,1536]{1,0:T(8,128)(2,1)S(1)}, u32[]{:S(2)}, u32[]{:S(2)}) collective-permute-start(bf16[16,1536]{1,0:T(8,128)(2,1)S(1)} %get-tuple-element.15), channel_id=1, source_target_pairs={{16,0},{32,16},{48,32},{64,48},{80,64},{96,80},{112,96},{17,1},{33... | collective-permute-start | bytes 147464 | tf_op jit(solution)/shard_map/ppermute | solution.py:307
Sparse Core Ops, SparseCore 0:
  9.1 55.5 all-gather.2
  66.4 102.5 all-gather.4

commit v2 on v0

v2 whole, which is shorter than its diff:
```python
import functools
import math

import jax
import jax.numpy as jnp
from jax import lax
from jax.experimental import pallas as pl
from jax.experimental.pallas import tpu as pltpu
from jax.sharding import PartitionSpec as P

HEADS = 8
HEAD = 96
KERNEL = 31
EPS = 1e-05
ROWS = 384
PAD = 16
SLOT = 12
RANKS = 128
D = 1536
F32 = jnp.float32
BF16 = jnp.bfloat16
VMEM = pltpu.VMEM
DMA = pltpu.SemaphoreType.DMA
MESH = pl.DeviceIdType.MESH
PARTS = 8
MIB = 1024 * 1024


def vspec():
    return pl.BlockSpec(memory_space=pltpu.VMEM)


def dot(a, b):
    return jnp.dot(a, b, preferred_element_type=F32)


def iota(shape, dim):
    return lax.broadcasted_iota(jnp.int32, shape, dim)


def layer_norm(values):
    row_mean = jnp.mean(values, axis=-1, keepdims=True)
    centred = values - row_mean
    variance = jnp.mean(centred * centred, axis=-1, keepdims=True)
    return (centred * lax.rsqrt(variance + EPS)).astype(BF16)


def remote(source, target, send, recv, device):
    return pltpu.make_async_remote_copy(
        src_ref=source, dst_ref=target, send_sem=send, recv_sem=recv, device_id=device, device_id_type=MESH
    )


class Gather:
    def __init__(self, own, full, split, send, recv, here):
        ctx, sess = here
        y, z_hi = ctx // 2, ctx % 2
        z_lo, x, core = sess // 8, (sess // 2) % 4, sess % 2
        z = 2 * z_hi + z_lo

        def device(x_at, z_at, core_at):
            return (2 * y + z_at // 2, (z_at % 2) * 8 + x_at * 2 + core_at)

        self.next, self.prev = device((x + 1) % 4, z, core), device((x + 3) % 4, z, core)
        self.above, self.below = device(x, (z + 1) % 4, core), device(x, (z + 3) % 4, core)
        self.twin = device(x, z, 1 - core)
        self.order = [x, (x + 3) % 4, (x + 1) % 4, (x + 2) % 4]
        self.index = lambda z_at, x_at, core_at: z_at * 8 + x_at * 2 + core_at
        self.z_lo, self.core, self.sess = z_lo, core, sess
        self.own, self.full = own, full
        rows = own.shape[0]
        self.low, self.high = pl.ds(0, split), pl.ds(split, rows - split)
        self.send_sem, self.recv_sem = send, recv
        self.sent = []

    def send(self, source, target, recv, device):
        copy = remote(source, target, self.send_sem.at[len(self.sent)], self.recv_sem.at[recv], device)
        copy.start()
        self.sent.append(copy)

    def pass_on(self, part, recv, device):
        self.send(part, part, recv, device)

    def wait(self, part, recv):
        remote(part, part, self.send_sem.at[0], self.recv_sem.at[recv], self.twin).wait_recv()

    def start(self):
        full, sess = self.full, self.sess
        self.send(self.own, full.at[sess], 0, self.next)
        self.send(self.own, full.at[sess], 1, self.prev)
        self.send(self.own.at[self.low], full.at[sess, self.low], 4, self.above)
        self.send(self.own.at[self.high], full.at[sess, self.high], 5, self.below)
        self.send(self.own, full.at[sess], 12, self.twin)

    def along_x(self):
        full, low, high = self.full, self.low, self.high
        a = self.index(self.z_lo, self.order[1], self.core)
        b = self.index(self.z_lo, self.order[2], self.core)
        self.wait(full.at[a], 0)
        self.pass_on(full.at[a, low], 2, self.next)
        self.wait(full.at[b], 1)
        self.pass_on(full.at[b, high], 3, self.prev)
        for at, recv in ((a, 6), (b, 8)):
            self.pass_on(full.at[at, low], recv, self.above)
            self.pass_on(full.at[at, high], recv + 1, self.below)
        self.pass_on(full.at[a], 13, self.twin)
        self.pass_on(full.at[b], 14, self.twin)

    def across(self):
        full, low, high = self.full, self.low, self.high
        c = self.index(self.z_lo, self.order[3], self.core)
        self.wait(full.at[c, low], 2)
        self.pass_on(full.at[c, low], 10, self.above)
        self.pass_on(full.at[c, low], 15, self.twin)
        self.wait(full.at[c, high], 3)
        self.pass_on(full.at[c, high], 11, self.below)
        self.pass_on(full.at[c, high], 16, self.twin)

    def along_z(self, which):
        full, low, high = self.full, self.low, self.high
        for j in which:
            at = self.index(1 - self.z_lo, self.order[j], self.core)
            self.wait(full.at[at, low], 4 + 2 * j)
            self.pass_on(full.at[at, low], 17 + 2 * j, self.twin)
            self.wait(full.at[at, high], 5 + 2 * j)
            self.pass_on(full.at[at, high], 18 + 2 * j, self.twin)

    def finish(self):
        full, low, high, core = self.full, self.low, self.high, 1 - self.core
        for j in range(3):
            self.wait(full.at[self.index(self.z_lo, self.order[j], core)], 12 + j)
        at = self.index(self.z_lo, self.order[3], core)
        self.wait(full.at[at, low], 15)
        self.wait(full.at[at, high], 16)
        for j in range(4):
            at = self.index(1 - self.z_lo, self.order[j], core)
            self.wait(full.at[at, low], 17 + 2 * j)
            self.wait(full.at[at, high], 18 + 2 * j)

    def drain(self):
        for copy in self.sent:
            copy.wait_send()


GATHER_SENDS = 25
GATHER_RECVS = 25


def merged(block):
    return block.reshape(block.shape[0] * block.shape[1], block.shape[2])


def block_kernel(
    live_rows, slots, first, second, kernel, lin_hbm, qkv_own, tail_own,
    out, tail_full,
    arrived, wide, sorted_rows, frames, halo, last, sel, win_e, win_o, band, taps,
    even, odd, behind, sub, big, emb, normed, w_qkv, sent, held, context, heads,
    residual, gated, edges, deep,
    mel_send, mel_recv, local_sem, halo_send, halo_recv,
    qkv_send, qkv_recv, head_send, head_recv, edge_send, edge_recv,
    gq_send, gq_recv, gt_send, gt_recv,
):
    ctx, sess = lax.axis_index("ctx"), lax.axis_index("sess")
    me = ctx * 16 + sess
    total = ROWS + PAD
    here = (ctx, sess)
    after, before = ((ctx + 1) % PARTS, sess), ((ctx + PARTS - 1) % PARTS, sess)

    barrier = pltpu.get_barrier_semaphore()

    def greet(i, carry):
        other = lax.rem(me + i, RANKS)
        pl.semaphore_signal(barrier, inc=1, device_id=(other // 16, other % 16), device_id_type=MESH)
        return carry

    lax.fori_loop(1, RANKS, greet, 0)
    lin_copy = pltpu.make_async_copy(lin_hbm, big, local_sem.at[0])
    lin_copy.start()
    own_qkv = pltpu.make_async_copy(qkv_own, w_qkv.at[sess], local_sem.at[1])
    own_qkv.start()
    own_tail = pltpu.make_async_copy(tail_own, tail_full.at[sess], local_sem.at[2])
    own_tail.start()
    own_slot = pltpu.make_async_copy(slots.at[me], arrived.at[me], local_sem.at[3])
    own_slot.start()
    prepare(first, second, sel, band, taps)
    pl.semaphore_wait(barrier, RANKS - 1)

    def deliver(i, carry):
        other = lax.rem(me + i, RANKS)
        remote(slots.at[other], arrived.at[me], mel_send, mel_recv, (other // 16, other % 16)).start()
        return carry

    lax.fori_loop(1, RANKS, deliver, 0)
    gather_qkv = Gather(qkv_own, w_qkv, 48, gq_send, gq_recv, here)
    gather_tail = Gather(tail_own, tail_full, 128, gt_send, gt_recv, here)
    gather_qkv.start()
    own_slot.wait()
    all_slots = remote(slots.at[0 : RANKS - 1], arrived.at[0 : RANKS - 1], mel_send, mel_recv, after)
    all_slots.wait_recv()

    place(arrived, wide, sorted_rows, frames)
    halo_copy = remote(frames.at[ROWS - PAD :], halo, halo_send, halo_recv, after)
    halo_copy.start()
    gather_qkv.along_x()
    win_o[PAD:total, :] = dot(frames[:, 128:512], sel[...]).astype(BF16)
    halo_copy.wait_recv()
    first_rows = jnp.where(ctx > 0, halo[...].astype(F32), 0.0)
    last[0:PAD, :] = first_rows[:, 384:512]
    last[PAD:total, :] = frames[:, 384:512].astype(F32)
    previous = last[pl.ds(PAD - 1, ROWS), :].astype(BF16)
    win_e[...] = dot(jnp.concatenate([previous, frames[:, 0:256]], axis=1), sel[...]).astype(BF16)
    win_o[0:PAD, :] = dot(first_rows.astype(BF16)[:, 128:512], sel[...]).astype(BF16)

    def four_bins(g, side):
        q = pl.multiple_of((g // 4) * 128, 128)
        weights = band[:, pl.ds(pl.multiple_of((g % 4) * 512, 512), 512)]
        even[side, :, 128:640] = jnp.maximum(dot(win_e[:, pl.ds(q, 128)], weights), 0.0).astype(BF16)
        odd[side, :, 128:640] = jnp.maximum(dot(win_o[:, pl.ds(q, 128)], weights), 0.0).astype(BF16)
        even[1 - side, :, 0:128] = even[side, :, 512:640]
        odd[1 - side, :, 0:128] = odd[side, :, 512:640]

    def two_bins(g, side):
        behind[...] = dot(odd[side], taps[1280:1920, :])
        both = jnp.concatenate([even[side], odd[side, PAD:total, :]], axis=1)
        rows = dot(both, taps[0:1280, :]) + behind[pl.ds(PAD - 1, ROWS), :]
        sub[:, pl.ds(pl.multiple_of(g * 256, 256), 256)] = jnp.maximum(rows, 0.0).astype(BF16)

    def groups(i, carry):
        four_bins(2 * i, 0)
        two_bins(2 * i, 0)
        four_bins(2 * i + 1, 1)
        two_bins(2 * i + 1, 1)
        return carry

    even[0, :, 0:128] = jnp.zeros((ROWS, 128), BF16)
    odd[0, :, 0:128] = jnp.zeros((total, 128), BF16)
    lax.fori_loop(0, 3, groups, 0)
    gather_qkv.across()
    gather_tail.start()
    lax.fori_loop(3, 6, groups, 0)
    gather_qkv.along_z((0, 1))
    lax.fori_loop(6, 8, groups, 0)
    gather_qkv.along_z((2, 3))
    lin_copy.wait()

    def project(n, carry):
        at = pl.multiple_of(n * 512, 512)
        emb[:, pl.ds(at, 512)] = dot(sub[...], merged(big[:, :, pl.ds(at, 512)])).astype(BF16)
        return carry

    lax.fori_loop(0, 3, project, 0)
    normed[...] = layer_norm(emb[...].astype(F32))
    gather_tail.along_x()

    gather_qkv.finish()
    own_qkv.wait()
    lane = iota((ROWS, 128), 1)
    live = iota((ROWS, 128), 0) < live_rows[0]
    shares = []
    for part in (1, 2, 0):
        rows = dot(normed[...], merged(w_qkv[:, :, 768 * part : 768 * (part + 1)]))
        if part == 1:
            extra = jnp.where(live, 0.0, -1e30)
        else:
            extra = jnp.ones((ROWS, 128), F32)
        for h in range(HEADS):
            base, shift = (96 * h) // 128 * 128, (96 * h) % 128
            if shift == 0:
                head = rows[:, base : base + 128]
            elif shift == 32:
                head = pltpu.roll(rows[:, base : base + 128], 128 - shift, 1)
            else:
                head = pltpu.roll(rows[:, base : base + 256], 256 - shift, 1)[:, 0:128]
            head = jnp.where(lane < HEAD, head, jnp.where(lane == HEAD, extra, 0.0))
            sent[part, h] = head.astype(BF16)
        own = pltpu.make_async_copy(sent.at[part, ctx], held.at[part, ctx], local_sem.at[4 + part])
        own.start()
        shares.append(own)
        for i in range(1, PARTS):
            other = lax.rem(ctx + i, PARTS)
            copy = remote(
                sent.at[part, other], held.at[part, ctx],
                qkv_send.at[part, i], qkv_recv.at[part, i], (other, sess),
            )
            copy.start()
            shares.append(copy)
    gather_tail.across()
    tail_copy = pltpu.make_async_copy(tail_full, big.at[:, 0:240, :], local_sem.at[7])
    for copy in shares:
        copy.wait()
    gather_tail.along_z((0, 1))

    scale = math.log2(math.e) / math.sqrt(HEAD)

    def attend(i, carry):
        other = lax.rem(ctx + i, PARTS)
        keys, values = merged(held[1]), merged(held[2])
        for half in range(2):
            at = pl.ds(half * (ROWS // 2), ROWS // 2)
            scores = lax.dot_general(
                held[0, other, at, :], keys, (((1,), (1,)), ((), ())), preferred_element_type=F32
            )
            row_max = jnp.max(scores, axis=1, keepdims=True)
            weights = jnp.exp2((scores - row_max) * scale).astype(BF16)
            summed = dot(weights, values)
            result = summed / summed[:, HEAD : HEAD + 1]
            result = jnp.where(iota(result.shape, 1) < HEAD, result, 0.0)
            context[other, at, :] = result.astype(BF16)
        return carry

    def attend_for(i, carry):
        attend(i, carry)
        other = lax.rem(ctx + i, PARTS)
        remote(
            context.at[other], heads.at[ctx], head_send.at[i], head_recv.at[i], (other, sess)
        ).start()
        return carry

    lax.fori_loop(1, 5, attend_for, 0)
    gather_tail.along_z((2, 3))
    lax.fori_loop(5, PARTS, attend_for, 0)
    gather_tail.finish()
    own_tail.wait()
    tail_copy.start()
    attend(0, 0)
    own = pltpu.make_async_copy(context.at[ctx], heads.at[ctx], local_sem.at[8])
    own.start()
    own.wait()
    for i in range(1, PARTS):
        other = lax.rem(ctx + i, PARTS)
        remote(context.at[other], heads.at[ctx], head_send.at[i], head_recv.at[i], (other, sess)).wait()
    tail_copy.wait()

    w_out = merged(big[:, 192:240, :])
    summed = emb[...].astype(F32)
    for pair in range(4):
        left = jnp.concatenate([heads[2 * pair], heads[2 * pair + 1]], axis=1)
        at = 192 * pair
        pad = jnp.zeros((32, D), BF16)
        right = jnp.concatenate([w_out[at : at + 96], pad, w_out[at + 96 : at + 192], pad], axis=0)
        summed = summed + dot(left, right)
    residual[...] = summed.astype(BF16)
    normed[...] = layer_norm(residual[...].astype(F32))
    live = iota((ROWS, 256), 0) < live_rows[0]

    def lift(n, carry):
        at = pl.ds(pl.multiple_of(n * 256, 256), 256)
        value = dot(normed[...], merged(big[:, 0:96, at]))
        gate = dot(normed[...], merged(big[:, 96:192, at]))
        rows = jnp.where(live, value * jax.nn.sigmoid(gate), 0.0).astype(BF16)
        gated[:, at] = rows
        deep[PAD : PAD + ROWS, at] = rows.astype(F32)
        return carry

    lax.fori_loop(0, 6, lift, 0)
    to_after = remote(gated.at[ROWS - PAD :], edges.at[0], edge_send.at[0], edge_recv.at[0], after)
    to_before = remote(gated.at[0:PAD], edges.at[1], edge_send.at[1], edge_recv.at[1], before)
    to_after.start()
    to_before.start()

    def taps_of(n, starts):
        at = pl.ds(pl.multiple_of(n * 128, 128), 128)
        weights = kernel[:, at].astype(F32)
        for start in starts:
            rows = jnp.zeros((64, 128), F32)
            for j in range(KERNEL):
                rows = rows + deep[pl.ds(start + j + 1, 64), at] * weights[j : j + 1, :]
            rows = residual[start : start + 64, at].astype(F32) + rows * jax.nn.sigmoid(rows)
            out[start : start + 64, at] = rows.astype(BF16)

    def inner(n, carry):
        taps_of(n, (64, 128, 192, 256))
        return carry

    def outer(n, carry):
        taps_of(n, (0, 320))
        return carry

    lax.fori_loop(0, D // 128, inner, 0)
    to_after.wait_recv()
    to_before.wait_recv()
    deep[0:PAD, :] = jnp.where(ctx > 0, edges[0].astype(F32), 0.0)
    deep[PAD + ROWS :, :] = jnp.where(ctx < PARTS - 1, edges[1].astype(F32), 0.0)
    lax.fori_loop(0, D // 128, outer, 0)

    all_slots.wait_send()
    halo_copy.wait_send()
    to_after.wait_send()
    to_before.wait_send()
    gather_qkv.drain()
    gather_tail.drain()


def prepare(first, second, sel, band, taps):
    row = iota((384, 512), 0)
    col = iota((384, 512), 1)
    a, m, p, r = row // 128, row % 128, col // 32, col % 32
    b = jnp.where(r >= 9, 1, 0) + jnp.where(r >= 18, 1, 0)
    hit = (r < 27) & (a == b) & (m == 8 * p - 1 + r - 9 * b)
    sel[...] = jnp.where(hit, 1.0, 0.0).astype(BF16)
    band_row = iota((128, 128), 0)
    values = first[...].astype(F32)
    for f in range(16):
        block = jnp.zeros((128, 128), F32)
        for tap in range(9):
            at = 32 * (f // 4) + 9 * (tap // 3) + 2 * (f % 4) + tap % 3
            block = jnp.where(band_row == at, values[tap : tap + 1, :], block)
        band[:, 128 * f : 128 * (f + 1)] = block.astype(BF16)
    taps[...] = jnp.zeros_like(taps)
    for position, row_tap in enumerate((1, 2, 0)):
        for o in range(2):
            for c in range(3):
                at = 640 * position + 128 * (2 * o + c)
                source = (3 * row_tap + c) * 128
                taps[at : at + 128, 128 * o : 128 * (o + 1)] = second[source : source + 128, :]


def place(arrived, wide, sorted_rows, frames):
    wide[...] = merged(arrived[...]).astype(F32)
    high = wide[pl.ds(SLOT, RANKS, stride=16), :]
    low = wide[pl.ds(SLOT + 1, RANKS, stride=16), :]
    position = (high * 64.0 + low).T
    for r in range(SLOT):
        sorted_rows[r * RANKS : (r + 1) * RANKS, :] = wide[pl.ds(r, RANKS, stride=16), :].astype(BF16)
    target = iota((ROWS, RANKS), 0).astype(F32) * 4.0
    for k in range(4):
        chosen = jnp.concatenate(
            [
                jnp.where(position[r : r + 1, :] == target + float(k), 1.0, 0.0).astype(BF16)
                for r in range(SLOT)
            ],
            axis=1,
        )
        frames[:, 128 * k : 128 * (k + 1)] = dot(chosen, sorted_rows[...]).astype(BF16)


def block(live_rows, slots, first, second, kernel, lin_in, qkv_own, tail_own):
    total = ROWS + PAD
    anywhere = pl.BlockSpec(memory_space=pl.ANY)
    return pl.pallas_call(
        block_kernel,
        out_shape=[
            jax.ShapeDtypeStruct((ROWS, D), BF16),
            jax.ShapeDtypeStruct((16, 240, D), BF16),
        ],
        in_specs=[pl.BlockSpec(memory_space=pltpu.SMEM)] + [vspec()] * 4 + [anywhere] * 3,
        out_specs=[vspec(), anywhere],
        scratch_shapes=[
            VMEM((RANKS, 16, 128), BF16),
            VMEM((16 * RANKS, 128), F32),
            VMEM((SLOT * RANKS, 128), BF16),
            VMEM((ROWS, 512), BF16),
            VMEM((PAD, 512), BF16),
            VMEM((total, 128), F32),
            VMEM((384, 512), BF16),
            VMEM((ROWS, 512), BF16),
            VMEM((total, 512), BF16),
            VMEM((128, 2048), BF16),
            VMEM((1920, 256), BF16),
            VMEM((2, ROWS, 640), BF16),
            VMEM((2, total, 640), BF16),
            VMEM((total, 256), F32),
            VMEM((ROWS, 4096), BF16),
            VMEM((16, 256, D), BF16),
            VMEM((ROWS, D), BF16),
            VMEM((ROWS, D), BF16),
            VMEM((16, 96, 2304), BF16),
            VMEM((3, HEADS, ROWS, 128), BF16),
            VMEM((3, HEADS, ROWS, 128), BF16),
            VMEM((HEADS, ROWS, 128), BF16),
            VMEM((HEADS, ROWS, 128), BF16),
            VMEM((ROWS, D), BF16),
            VMEM((ROWS, D), BF16),
            VMEM((2, PAD, D), BF16),
            VMEM((ROWS + 2 * PAD, D), F32),
            DMA, DMA, DMA((9,)), DMA, DMA,
            DMA((3, PARTS)), DMA((3, PARTS)), DMA((PARTS,)), DMA((PARTS,)), DMA((2,)), DMA((2,)),
            DMA((GATHER_SENDS,)), DMA((GATHER_RECVS,)), DMA((GATHER_SENDS,)), DMA((GATHER_RECVS,)),
        ],
        compiler_params=pltpu.CompilerParams(
            vmem_limit_bytes=62 * MIB, collective_id=0, has_side_effects=True
        ),
        cost_estimate=pl.CostEstimate(
            flops=27_000_000_000, bytes_accessed=60_000_000, transcendentals=12_000_000
        ),
        name="conformer_block",
    )(live_rows, slots, first, second, kernel, lin_in, qkv_own, tail_own)


def local(mel_in, route, lengths, conv_first, conv_second, lin_in, wq, wk, wv, wo, pw1, dw_kernel):
    qkv_own = jnp.concatenate([wq, wk, wv], axis=1)
    tail_own = jnp.concatenate([pw1[:, :D], pw1[:, D:], wo], axis=0)
    position = jnp.pad(route.reshape(RANKS, 1, SLOT), ((0, 0), (0, 0), (0, 128 - SLOT)))
    slots = jnp.concatenate(
        [
            mel_in.reshape(RANKS, SLOT, 128),
            (position // 64).astype(BF16),
            (position % 64).astype(BF16),
            jnp.zeros((RANKS, 2, 128), BF16),
        ],
        axis=1,
    )
    first = jnp.pad(conv_first, ((0, 7), (0, 0)))
    kernel = jnp.pad(dw_kernel, ((0, 1), (0, 0)))
    length = lengths[lax.axis_index("sess")]
    live_rows = (length - lax.axis_index("ctx") * ROWS).reshape(1)
    encoded, _ = block(
        live_rows, slots, first, conv_second, kernel, lin_in.reshape(16, 256, D), qkv_own, tail_own
    )
    return encoded[None]


def solution(mesh):
    return jax.shard_map(
        local,
        mesh=mesh,
        in_specs=(
            P(("ctx", "sess"), None),
            P(("ctx", "sess")),
            P(),
            P(),
            P(),
            P(),
            P("sess", None),
            P("sess", None),
            P("sess", None),
            P("sess", None),
            P("sess", None),
            P(),
        ),
        out_specs=P("sess", "ctx", None),
        check_vma=False,
    )
```

time: 473 us -> 155 us (0.33)
  the two profiles are of different devices: /device:TPU:0 before, /device:TPU:1 now
where the time goes in v2:
time: 155 us; the launch traced here: 153 us
  Pallas kernels  140 us (90%)
  local copies, waits for them, and re-layouts  7.49 us (5%)
  other arithmetic  4.59 us (3%)
    pallas_call x1, Pallas kernels, block(): pl.pallas_call(block_kernel, out_shape=[jax.ShapeDtypeStruct((ROWS, D), B...  140 us

profile of v2, /device:TPU:1, one launch (start us, length us, event | category | flops | bytes accessed | tf_op | source)
XLA Modules:
  0.0 152.6 jit_solution(3594590949619839485)
XLA Ops:
  0.0 0.0 copy-start.1
  0.0 1.3 dynamic_slice.3
  2.0 0.1 pad.24.clone
  2.0 1.3 pad.13.first
  3.3 0.8 reshape.14
  4.1 0.3 fusion.1
  4.5 0.1 fusion
  4.6 1.5 %pad.14.kernel = bf16[32,1536]{1,0:T(8,128)(2,1)} pad(bf16[31,1536]{1,0:T(8,128)(2,1)} %param.23, bf16[]{:T(256)} %constant.44.clone.1), padding=0_1x0_0 | pad | bytes 193538 | tf_op jit(solution)/shard_map/jit(_pad)/pad | solution.py:504
  6.1 0.0 copy-start
  6.1 1.9 %pad_maximum_fusion.1.qkv_own = bf16[96,2304]{1,0:T(8,128)(2,1)} fusion(bf16[96,768]{1,0:T(8,128)(2,1)} %param.20, bf16[96,768]{1,0:T(8,128)(2,1)} %param.19, bf16[96,768]{1,0:T(8,128)(2,1)} %param.18), kind=kLoop, calls=%fused_computation.2 | loop fusion | flops 1327104 | bytes 884736 | tf_op jit(solution)/shard_map/concatenate | solution.py:491
  8.0 0.0 copy-done.1
  8.1 0.0 copy-start.2
  8.1 0.1 reshape.13
  8.1 1.3 maximum_maximum_fusion.slots
  9.5 0.0 copy-done
  9.5 0.0 copy-done.2
  9.5 0.9 pad_maximum_fusion.tail_own
  10.4 139.8 %conformer_block.1 = (bf16[384,1536]{1,0:T(8,128)(2,1)}, bf16[16,240,1536]{2,1,0:T(8,128)(2,1)}) custom-call(s32[1]{0:T(128)} %bitcast.1.live_rows, bf16[128,16,128]{2,1,0:T(8,128)(2,1)} %maximum_maximum_fusion.slots, bf16[16,128]{1,0:T(8,128)(2,1)} %pad.13.first, bf16[1152,128]{1,0:T(8,128)(2,1)} %second.1, bf16[32,1536]{1,0:T(8,128)(2,1)} %pad.14.kernel, ...), custom_call_target="tpu_custom_call" | custom-call | flops 27000000512 | bytes 60000000 | tf_op jit(solution)/shard_map/conformer_block/pallas_call | solution.py:440
  150.2 2.4 %copy.15 = bf16[1,384,1536]{2,1,0:T(8,128)(2,1)} copy(bf16[1,384,1536]{2,1,0:T(8,128)(2,1)} %bitcast.5) | data formatting | bytes 2359296
  (2 shorter events, 0.0 us)
Async XLA Ops:
  0.0 8.1 %copy-start.1 = (bf16[1536,128]{1,0:T(8,128)(2,1)S(1)}, bf16[1536,128]{1,0:T(8,128)(2,1)}, u32[]{:S(2)}) copy-start(bf16[1536,128]{1,0:T(8,128)(2,1)} %param.12) | copy-start | bytes 1179652
  6.1 3.3 %copy-start = (bf16[96,3072]{1,0:T(8,128)(2,1)S(1)}, bf16[96,3072]{1,0:T(8,128)(2,1)}, u32[]{:S(2)}) copy-start(bf16[96,3072]{1,0:T(8,128)(2,1)} %param.22) | copy-start | bytes 1769476
  8.1 1.4 copy-start.2

commit v3 on v2

v3 whole, which is shorter than its diff:
```python
import functools
import math

import jax
import jax.numpy as jnp
from jax import lax
from jax.experimental import pallas as pl
from jax.experimental.pallas import tpu as pltpu
from jax.sharding import PartitionSpec as P

HEADS = 8
HEAD = 96
KERNEL = 31
EPS = 1e-05
ROWS = 384
PAD = 16
SLOT = 12
RANKS = 128
D = 1536
F32 = jnp.float32
BF16 = jnp.bfloat16
VMEM = pltpu.VMEM
DMA = pltpu.SemaphoreType.DMA
MESH = pl.DeviceIdType.MESH
PARTS = 8
HALF = ROWS // 2
MIB = 1024 * 1024


def vspec():
    return pl.BlockSpec(memory_space=pltpu.VMEM)


def dot(a, b):
    return jnp.dot(a, b, preferred_element_type=F32)


def iota(shape, dim):
    return lax.broadcasted_iota(jnp.int32, shape, dim)


def layer_norm(values):
    row_mean = jnp.mean(values, axis=-1, keepdims=True)
    centred = values - row_mean
    variance = jnp.mean(centred * centred, axis=-1, keepdims=True)
    return (centred * lax.rsqrt(variance + EPS)).astype(BF16)


def remote(source, target, send, recv, device):
    return pltpu.make_async_remote_copy(
        src_ref=source, dst_ref=target, send_sem=send, recv_sem=recv, device_id=device, device_id_type=MESH
    )


class Gather:
    def __init__(self, full, base, rows, split, send, recv, here):
        ctx, sess = here
        y, z_hi = ctx // 2, ctx % 2
        z_lo, x, core = sess // 8, (sess // 2) % 4, sess % 2
        z, odd = 2 * z_hi + z_lo, y % 2

        def device(x_at, y_at, z_at, core_at):
            return (2 * y_at + z_at // 2, (z_at % 2) * 8 + x_at * 2 + core_at)

        self.next, self.prev = device((x + 1) % 4, y, z, core), device((x + 3) % 4, y, z, core)
        self.above, self.below = device(x, y, (z + 1) % 4, core), device(x, y, (z + 3) % 4, core)
        self.front, self.back = device(x, (y + 1) % 4, z, core), device(x, (y + 3) % 4, z, core)
        self.twin = device(x, y, z, 1 - core)
        near = [x, (x + 3) % 4, (x + 1) % 4, (x + 2) % 4]
        mine = [near[0] * (1 - odd) + near[2] * odd, near[1] * (1 - odd) + near[3] * odd]
        theirs = [near[0] * odd + near[2] * (1 - odd), near[1] * odd + near[3] * (1 - odd)]
        at = lambda z_at, x_at, core_at: z_at * 8 + x_at * 2 + core_at
        self.own = sess
        self.a, self.b, self.c = (at(z_lo, i, core) for i in near[1:])
        self.give = [at(z_lo, i, core) for i in mine]
        self.take = [at(1 - z_lo, i, core) for i in mine]
        self.from_y = [at(1 - z_lo, i, core) for i in theirs]
        self.from_twin = (
            [at(z_lo, i, 1 - core) for i in near]
            + [at(1 - z_lo, i, 1 - core) for i in mine]
            + [at(1 - z_lo, i, 1 - core) for i in theirs]
        )
        self.other = [at(1 - z_lo, i, core) for i in near]
        self.twin_order = [at(z, i, 1 - core) for z in (z_lo, 1 - z_lo) for i in near]
        self.full = full
        self.all = pl.ds(base, rows)
        self.low, self.high = pl.ds(base, split), pl.ds(base + split, rows - split)
        self.send_sem, self.recv_sem = send, recv
        self.sent = []

    def copy(self, shard, rows, number, recv, device):
        part = self.full.at[shard, rows]
        return remote(part, part, self.send_sem.at[number], self.recv_sem.at[recv], device)

    def send(self, shard, rows, recv, device):
        what = (shard, rows, len(self.sent), recv, device)
        self.copy(*what).start()
        self.sent.append(what)

    def wait(self, shard, rows, recv):
        self.copy(shard, rows, 0, recv, self.twin).wait_recv()

    def start(self):
        self.send(self.own, self.all, 0, self.next)
        self.send(self.own, self.all, 1, self.prev)
        self.send(self.own, self.all, 12, self.twin)

    def along_x(self):
        self.wait(self.a, self.all, 0)
        self.send(self.a, self.low, 2, self.next)
        self.wait(self.b, self.all, 1)
        self.send(self.b, self.high, 3, self.prev)
        self.send(self.give[0], self.low, 4, self.above)
        self.send(self.give[0], self.high, 5, self.below)
        self.send(self.a, self.all, 13, self.twin)
        self.send(self.b, self.all, 14, self.twin)

    def across(self):
        self.wait(self.c, self.low, 2)
        self.wait(self.c, self.high, 3)
        self.send(self.give[1], self.low, 6, self.above)
        self.send(self.give[1], self.high, 7, self.below)
        self.send(self.c, self.all, 15, self.twin)

    def along_z(self, k):
        self.wait(self.take[k], self.low, 4 + 2 * k)
        self.send(self.take[k], self.low, 16 + 2 * k, self.front)
        self.wait(self.take[k], self.high, 5 + 2 * k)
        self.send(self.take[k], self.high, 17 + 2 * k, self.back)
        self.send(self.take[k], self.all, 8 + k, self.twin)

    def along_y(self):
        for k in range(2):
            self.wait(self.from_y[k], self.low, 16 + 2 * k)
            self.wait(self.from_y[k], self.high, 17 + 2 * k)
            self.send(self.from_y[k], self.all, 10 + k, self.twin)

    def finish(self):
        for shard, recv in zip(self.from_twin, (12, 13, 14, 15, 8, 9, 10, 11)):
            self.wait(shard, self.all, recv)

    def drain(self):
        for what in self.sent:
            self.copy(*what).wait_send()


class GatherAlongX(Gather):
    def begin(self):
        self.send(self.own, self.low, 0, self.above)
        self.send(self.own, self.high, 1, self.below)
        self.send(self.own, self.all, 10, self.twin)

    def start(self):
        self.send(self.own, self.all, 2, self.next)
        self.send(self.own, self.all, 3, self.prev)

    def start_other(self):
        z = self.other
        self.wait(z[0], self.low, 0)
        self.wait(z[0], self.high, 1)
        self.send(z[0], self.all, 4, self.next)
        self.send(z[0], self.all, 5, self.prev)
        self.send(z[0], self.all, 11, self.twin)

    def along_x(self, k):
        a, b = (self.a, self.b) if k == 0 else self.other[1:3]
        self.wait(a, self.all, 2 + 2 * k)
        self.send(a, self.low, 6 + 2 * k, self.next)
        self.wait(b, self.all, 3 + 2 * k)
        self.send(b, self.high, 7 + 2 * k, self.prev)
        self.send(a, self.all, 12 + 2 * k, self.twin)
        self.send(b, self.all, 13 + 2 * k, self.twin)

    def across(self, k):
        c = self.c if k == 0 else self.other[3]
        self.wait(c, self.low, 6 + 2 * k)
        self.wait(c, self.high, 7 + 2 * k)
        self.send(c, self.all, 16 + k, self.twin)

    def finish(self):
        for shard, recv in zip(self.twin_order, (10, 12, 13, 16, 11, 14, 15, 17)):
            self.wait(shard, self.all, recv)


GATHER_SENDS = 21
GATHER_RECVS = 20


def merged(block):
    return block.reshape(block.shape[0] * block.shape[1], block.shape[2])


def block_kernel(
    lengths, mel, route, first, second, kernel, lin_hbm, wq, wk, wv, wo, pw1,
    out, tail_full,
    mel_wide, high, low, slots, arrived, wide, turned, sorted_rows, frames, halo, last, sel, win_e, win_o,
    band, taps, even, odd, behind, sub, big, emb, normed, w_q, w_k, w_v, sent, held, context, heads, tail_own,
    residual, gated, edges, deep,
    mel_send, mel_recv, local_sem, halo_send, halo_recv,
    qkv_send, qkv_recv, head_send, head_recv, edge_send, edge_recv, gather_send, gather_recv,
):
    ctx, sess = lax.axis_index("ctx"), lax.axis_index("sess")
    me = ctx * 16 + sess
    total = ROWS + PAD
    here = (ctx, sess)
    after, before = ((ctx + 1) % PARTS, sess), ((ctx + PARTS - 1) % PARTS, sess)
    live_rows = lengths[sess] - ctx * ROWS

    barrier = pltpu.get_barrier_semaphore()

    def greet(i, carry):
        other = lax.rem(me + i, RANKS)
        pl.semaphore_signal(barrier, inc=1, device_id=(other // 16, other % 16), device_id_type=MESH)
        return carry

    lax.fori_loop(1, RANKS, greet, 0)
    own_copies = [
        pltpu.make_async_copy(source, target, local_sem.at[i])
        for i, (source, target) in enumerate(
            [
                (wk, w_k.at[sess]),
                (wv, w_v.at[sess]),
                (wq, w_q.at[sess]),
                (pw1.at[:, 0:D], tail_own.at[0:96]),
                (pw1.at[:, D : 2 * D], tail_own.at[96:192]),
                (wo, tail_own.at[192:240]),
                (lin_hbm, big),
            ]
        )
    ]
    for copy in own_copies:
        copy.start()
    lin_copy = own_copies[6]
    pack_slots(mel, route, mel_wide, high, low, wide, slots)
    own_slot = pltpu.make_async_copy(slots.at[me], arrived.at[me], local_sem.at[7])
    own_slot.start()
    prepare(first, second, sel, band, taps)
    gather_k, gather_v, gather_q, gather_t = (
        kind(full, base, rows, split, gather_send.at[i], gather_recv.at[i], here)
        for i, (kind, full, base, rows, split) in enumerate(
            [
                (Gather, w_k, 0, 96, 48),
                (Gather, w_v, 0, 96, 48),
                (Gather, w_q, 0, 96, 48),
                (GatherAlongX, tail_full, 0, 240, 128),
            ]
        )
    )
    for copy in own_copies[:6]:
        copy.wait()
    own_tail = pltpu.make_async_copy(tail_own, tail_full.at[sess], local_sem.at[3])
    own_tail.start()
    pl.semaphore_wait(barrier, RANKS - 1)
    gather_k.start()
    gather_v.start()
    gather_q.start()

    def deliver(i, carry):
        other = lax.rem(me + i, RANKS)
        remote(slots.at[other], arrived.at[me], mel_send, mel_recv, (other // 16, other % 16)).start()
        return carry

    lax.fori_loop(1, RANKS, deliver, 0)
    own_slot.wait()
    own_tail.wait()
    gather_t.begin()
    all_slots = remote(slots.at[0 : RANKS - 1], arrived.at[0 : RANKS - 1], mel_send, mel_recv, after)
    all_slots.wait_recv()

    place(me, arrived, wide, turned, sorted_rows, frames)
    halo_copy = remote(frames.at[ROWS - PAD :], halo, halo_send, halo_recv, after)
    halo_copy.start()
    gather_k.along_x()
    win_o[PAD:total, :] = dot(frames[:, 128:512], sel[...]).astype(BF16)
    halo_copy.wait_recv()
    first_rows = jnp.where(ctx > 0, halo[...].astype(F32), 0.0)
    last[0:PAD, :] = first_rows[:, 384:512]
    last[PAD:total, :] = frames[:, 384:512].astype(F32)
    previous = last[pl.ds(PAD - 1, ROWS), :].astype(BF16)
    win_e[...] = dot(jnp.concatenate([previous, frames[:, 0:256]], axis=1), sel[...]).astype(BF16)
    win_o[0:PAD, :] = dot(first_rows.astype(BF16)[:, 128:512], sel[...]).astype(BF16)
    gather_v.along_x()

    plan = [
        [gather_k.across, lambda: gather_k.along_z(0), gather_q.along_x],
        [gather_v.across, lambda: gather_v.along_z(0), gather_t.start],
        [gather_q.across, lambda: gather_q.along_z(0), lambda: gather_k.along_z(1)],
        [lambda: gather_v.along_z(1), gather_t.start_other],
        [lambda: gather_q.along_z(1), gather_k.along_y],
        [gather_v.along_y],
        [gather_q.along_y],
        [gather_k.finish, gather_v.finish],
    ]

    def four_bins(g, side):
        q = pl.ds(pl.multiple_of((g // 4) * 128, 128), 128)
        weights = band[:, pl.ds(pl.multiple_of((g % 4) * 512, 512), 512)]
        even[side, :, 128:640] = jnp.maximum(dot(win_e[:, q], weights), 0.0).astype(BF16)
        odd[side, :, 128:640] = jnp.maximum(dot(win_o[:, q], weights), 0.0).astype(BF16)
        even[1 - side, :, 0:128] = even[side, :, 512:640]
        odd[1 - side, :, 0:128] = odd[side, :, 512:640]

    def two_bins(g, side):
        behind[...] = dot(odd[side], taps[1280:1920, :])
        both = jnp.concatenate([even[side], odd[side, PAD:, :]], axis=1)
        rows = dot(both, taps[0:1280, :]) + behind[pl.ds(PAD - 1, ROWS), :]
        sub[:, pl.ds(pl.multiple_of(g * 256, 256), 256)] = jnp.maximum(rows, 0.0).astype(BF16)

    def groups(i, carry):
        four_bins(2 * i, 0)
        two_bins(2 * i, 0)
        four_bins(2 * i + 1, 1)
        two_bins(2 * i + 1, 1)
        for step, actions in enumerate(plan):

            @pl.when(i == step)
            def _():
                for action in actions:
                    action()

        return carry

    even[0, :, 0:128] = jnp.zeros((ROWS, 128), BF16)
    odd[0, :, 0:128] = jnp.zeros((total, 128), BF16)
    lax.fori_loop(0, 8, groups, 0)
    lin_copy.wait()

    def rows_of(half, carry):
        start = pl.multiple_of(half * HALF, HALF)
        mine = pl.ds(start, HALF)

        def project(n, carry):
            at = pl.ds(pl.multiple_of(n * 512, 512), 512)
            emb[mine, at] = dot(sub[mine, :], merged(big[:, :, at])).astype(BF16)
            return carry

        lax.fori_loop(0, 3, project, 0)
        normed[mine, :] = layer_norm(emb[mine, :].astype(F32))

        @pl.when(half == 0)
        def _():
            gather_q.finish()

        lane = iota((HALF, 128), 1)
        live = iota((HALF, 128), 0) < live_rows - start
        for part, weights in ((1, w_k), (2, w_v), (0, w_q)):
            rows = dot(normed[mine, :], merged(weights[...]))
            if part == 1:
                extra = jnp.where(live, 0.0, -1e30)
            else:
                extra = jnp.ones((HALF, 128), F32)
            for h in range(HEADS):
                base, shift = (96 * h) // 128 * 128, (96 * h) % 128
                if shift == 0:
                    head = rows[:, base : base + 128]
                elif shift == 32:
                    head = pltpu.roll(rows[:, base : base + 128], 128 - shift, 1)
                else:
                    head = pltpu.roll(rows[:, base : base + 256], 256 - shift, 1)[:, 0:128]
                head = jnp.where(lane < HEAD, head, jnp.where(lane == HEAD, extra, 0.0))
                sent[part, h, mine] = head.astype(BF16)
            own_share(half, part).start()

            def share(i, carry):
                share_of(half, part, i).start()
                return carry

            lax.fori_loop(1, PARTS, share, 0)
        return carry

    def own_share(half, part):
        mine = pl.ds(pl.multiple_of(half * HALF, HALF), HALF)
        return pltpu.make_async_copy(
            sent.at[part, ctx, mine], held.at[part, ctx, mine], local_sem.at[8 + 3 * half + part]
        )

    def share_of(half, part, i):
        mine = pl.ds(pl.multiple_of(half * HALF, HALF), HALF)
        other = lax.rem(ctx + i, PARTS)
        return remote(
            sent.at[part, other, mine], held.at[part, ctx, mine],
            qkv_send.at[half, part, i], qkv_recv.at[half, part, i], (other, sess),
        )

    lax.fori_loop(0, 2, rows_of, 0)
    gather_t.along_x(0)
    for half in range(2):
        for part in range(3):
            own_share(half, part).wait()
    for part in (1, 2):
        for half in range(2):

            def arrive(i, carry):
                share_of(half, part, i).wait_recv()
                return carry

            lax.fori_loop(1, PARTS, arrive, 0)

    scale = math.log2(math.e) / math.sqrt(HEAD)

    def attend(i):
        other = lax.rem(ctx + PARTS - i, PARTS)
        keys, values = merged(held[1]), merged(held[2])
        for half in range(2):
            at = pl.ds(half * HALF, HALF)
            scores = lax.dot_general(
                held[0, other, at, :], keys, (((1,), (1,)), ((), ())), preferred_element_type=F32
            )
            row_max = jnp.max(scores, axis=1, keepdims=True)
            weights = jnp.exp2((scores - row_max) * scale).astype(BF16)
            summed = dot(weights, values)
            result = summed / summed[:, HEAD : HEAD + 1]
            result = jnp.where(iota(result.shape, 1) < HEAD, result, 0.0)
            context[other, at, :] = result.astype(BF16)

    def head_of(i):
        other = lax.rem(ctx + PARTS - i, PARTS)
        return remote(
            context.at[other], heads.at[ctx], head_send.at[i], head_recv.at[i], (other, sess)
        )

    later = {
        3: [lambda: gather_t.along_x(1)],
        4: [lambda: gather_t.across(0)],
        7: [lambda: gather_t.across(1), gather_t.finish],
    }
    tail_copy = pltpu.make_async_copy(tail_full, big.at[:, 0:240, :], local_sem.at[14])
    later[7].append(tail_copy.start)

    def attend_for(i, carry):
        @pl.when(i < PARTS)
        def _():
            share_of(0, 0, i).wait_recv()
            share_of(1, 0, i).wait_recv()

        attend(i)

        @pl.when(i < PARTS)
        def _():
            head_of(i).start()

        for at, actions in later.items():

            @pl.when(i == at)
            def _():
                for action in actions:
                    action()

        return carry

    lax.fori_loop(1, PARTS + 1, attend_for, 0)
    own_head = pltpu.make_async_copy(context.at[ctx], heads.at[ctx], local_sem.at[15])
    own_head.start()
    own_head.wait()

    def arrive_heads(i, carry):
        head_of(i).wait()
        return carry

    lax.fori_loop(1, PARTS, arrive_heads, 0)
    tail_copy.wait()

    w_out = merged(big[:, 192:240, :])
    summed = emb[...].astype(F32)
    for pair in range(4):
        left = jnp.concatenate([heads[2 * pair], heads[2 * pair + 1]], axis=1)
        at = 192 * pair
        pad = jnp.zeros((32, D), BF16)
        right = jnp.concatenate([w_out[at : at + 96], pad, w_out[at + 96 : at + 192], pad], axis=0)
        summed = summed + dot(left, right)
    residual[...] = summed.astype(BF16)
    normed[...] = layer_norm(residual[...].astype(F32))
    live = iota((ROWS, 256), 0) < live_rows

    def lift(n, carry):
        at = pl.ds(pl.multiple_of(n * 256, 256), 256)
        value = dot(normed[...], merged(big[:, 0:96, at]))
        gate = dot(normed[...], merged(big[:, 96:192, at]))
        rows = jnp.where(live, value * jax.nn.sigmoid(gate), 0.0).astype(BF16)
        gated[:, at] = rows
        wide_rows = rows.astype(F32)
        deep[2 * n, PAD : PAD + ROWS, :] = wide_rows[:, 0:128]
        deep[2 * n + 1, PAD : PAD + ROWS, :] = wide_rows[:, 128:256]
        return carry

    lax.fori_loop(0, 6, lift, 0)
    to_after = remote(gated.at[ROWS - PAD :], edges.at[0], edge_send.at[0], edge_recv.at[0], after)
    to_before = remote(gated.at[0:PAD], edges.at[1], edge_send.at[1], edge_recv.at[1], before)
    to_after.start()
    to_before.start()

    def taps_of(n, starts):
        at = pl.ds(pl.multiple_of(n * 128, 128), 128)
        weights = kernel[:, at].astype(F32)
        for start in starts:
            rows = jnp.zeros((64, 128), F32)
            for j in range(KERNEL):
                rows = rows + deep[n, pl.ds(start + j + 1, 64), :] * weights[j : j + 1, :]
            rows = residual[start : start + 64, at].astype(F32) + rows * jax.nn.sigmoid(rows)
            out[start : start + 64, at] = rows.astype(BF16)

    def inner(n, carry):
        taps_of(n, (64, 128, 192, 256))
        return carry

    def outer(n, carry):
        at = pl.ds(pl.multiple_of(n * 128, 128), 128)
        deep[n, 0:PAD, :] = jnp.where(ctx > 0, edges[0, :, at].astype(F32), 0.0)
        deep[n, PAD + ROWS :, :] = jnp.where(ctx < PARTS - 1, edges[1, :, at].astype(F32), 0.0)
        taps_of(n, (0, 320))
        return carry

    lax.fori_loop(0, D // 128, inner, 0)
    to_after.wait_recv()
    to_before.wait_recv()
    lax.fori_loop(0, D // 128, outer, 0)

    all_slots.wait_send()
    halo_copy.wait_send()
    to_after.wait_send()
    to_before.wait_send()
    for half in range(2):
        for part in range(3):

            def leave(i, carry):
                share_of(half, part, i).wait_send()
                return carry

            lax.fori_loop(1, PARTS, leave, 0)
    for gather in (gather_k, gather_v, gather_q, gather_t):
        gather.drain()


def pack_slots(mel, route, mel_wide, high, low, wide, slots):
    mel_wide[...] = mel[...].astype(F32)
    high[...] = jnp.zeros_like(high)
    low[...] = jnp.zeros_like(low)
    high[0:SLOT, :] = (route[...] // 64).astype(F32)
    low[0:SLOT, :] = (route[...] % 64).astype(F32)

    def fill(j, carry):
        to = pl.multiple_of(16 * j, 16)
        at = (SLOT * j) // 128
        wide[pl.ds(to, SLOT), :] = mel_wide[pl.ds(SLOT * j, SLOT), :]
        wide[pl.ds(to + SLOT, 2), :] = high[pl.ds(at, 2), :]
        wide[pl.ds(to + SLOT + 2, 2), :] = low[pl.ds(at, 2), :]
        return carry

    lax.fori_loop(0, RANKS, fill, 0, unroll=8)
    slots[...] = wide[...].astype(BF16).reshape(RANKS, 16, 128)


def prepare(first, second, sel, band, taps):
    row = iota((384, 512), 0)
    col = iota((384, 512), 1)
    a, m, p, r = row // 128, row % 128, col // 32, col % 32
    b = jnp.where(r >= 9, 1, 0) + jnp.where(r >= 18, 1, 0)
    hit = (r < 27) & (a == b) & (m == 8 * p - 1 + r - 9 * b)
    sel[...] = jnp.where(hit, 1.0, 0.0).astype(BF16)
    band_row = iota((128, 128), 0)
    values = first[...].astype(F32)
    for f in range(16):
        block = jnp.zeros((128, 128), F32)
        for tap in range(9):
            at = 32 * (f // 4) + 9 * (tap // 3) + 2 * (f % 4) + tap % 3
            block = jnp.where(band_row == at, values[tap : tap + 1, :], block)
        band[:, 128 * f : 128 * (f + 1)] = block.astype(BF16)
    taps[...] = jnp.zeros_like(taps)
    for position, row_tap in enumerate((1, 2, 0)):
        for o in range(2):
            for c in range(3):
                at = 640 * position + 128 * (2 * o + c)
                source = (3 * row_tap + c) * 128
                taps[at : at + 128, 128 * o : 128 * (o + 1)] = second[source : source + 128, :]


def place(me, arrived, wide, turned, sorted_rows, frames):
    wide[...] = merged(arrived[...]).astype(F32)
    for k in range(2):
        high = wide[pl.ds(SLOT + k, RANKS, stride=16), :]
        low = wide[pl.ds(SLOT + 2 + k, RANKS, stride=16), :]
        turned[128 * k : 128 * (k + 1), :] = (high * 64.0 + low).T
    position = turned[pl.ds((SLOT * me) % 128, SLOT), :]
    for r in range(SLOT):
        sorted_rows[r * RANKS : (r + 1) * RANKS, :] = wide[pl.ds(r, RANKS, stride=16), :].astype(BF16)
    target = iota((ROWS, RANKS), 0).astype(F32) * 4.0
    for k in range(4):
        chosen = jnp.concatenate(
            [
                jnp.where(position[r : r + 1, :] == target + float(k), 1.0, 0.0).astype(BF16)
                for r in range(SLOT)
            ],
            axis=1,
        )
        frames[:, 128 * k : 128 * (k + 1)] = dot(chosen, sorted_rows[...]).astype(BF16)


def block(lengths, mel, route, first, second, kernel, lin_in, wq, wk, wv, wo, pw1):
    total = ROWS + PAD
    anywhere = pl.BlockSpec(memory_space=pl.ANY)
    return pl.pallas_call(
        block_kernel,
        out_shape=[
            jax.ShapeDtypeStruct((ROWS, D), BF16),
            jax.ShapeDtypeStruct((16, 240, D), BF16),
        ],
        in_specs=[pl.BlockSpec(memory_space=pltpu.SMEM)] + [vspec()] * 5 + [anywhere] * 6,
        out_specs=[vspec(), anywhere],
        scratch_shapes=[
            VMEM((RANKS * SLOT, 128), F32),
            VMEM((16, 128), F32),
            VMEM((16, 128), F32),
            VMEM((RANKS, 16, 128), BF16),
            VMEM((RANKS, 16, 128), BF16),
            VMEM((16 * RANKS, 128), F32),
            VMEM((256, 128), F32),
            VMEM((SLOT * RANKS, 128), BF16),
            VMEM((ROWS, 512), BF16),
            VMEM((PAD, 512), BF16),
            VMEM((total, 128), F32),
            VMEM((384, 512), BF16),
            VMEM((ROWS, 512), BF16),
            VMEM((total, 512), BF16),
            VMEM((128, 2048), BF16),
            VMEM((1920, 256), BF16),
            VMEM((2, ROWS, 640), BF16),
            VMEM((2, total, 640), BF16),
            VMEM((total, 256), F32),
            VMEM((ROWS, 4096), BF16),
            VMEM((16, 256, D), BF16),
            VMEM((ROWS, D), BF16),
            VMEM((ROWS, D), BF16),
            VMEM((16, 96, 768), BF16),
            VMEM((16, 96, 768), BF16),
            VMEM((16, 96, 768), BF16),
            VMEM((3, HEADS, ROWS, 128), BF16),
            VMEM((3, HEADS, ROWS, 128), BF16),
            VMEM((HEADS, ROWS, 128), BF16),
            VMEM((HEADS, ROWS, 128), BF16),
            VMEM((240, D), BF16),
            VMEM((ROWS, D), BF16),
            VMEM((ROWS, D), BF16),
            VMEM((2, PAD, D), BF16),
            VMEM((D // 128, ROWS + 2 * PAD, 128), F32),
            DMA, DMA, DMA((16,)), DMA, DMA,
            DMA((2, 3, PARTS)), DMA((2, 3, PARTS)), DMA((PARTS,)), DMA((PARTS,)), DMA((2,)), DMA((2,)),
            DMA((4, GATHER_SENDS)), DMA((4, GATHER_RECVS)),
        ],
        compiler_params=pltpu.CompilerParams(
            vmem_limit_bytes=62 * MIB, collective_id=0, has_side_effects=True
        ),
        cost_estimate=pl.CostEstimate(
            flops=27_000_000_000, bytes_accessed=60_000_000, transcendentals=12_000_000
        ),
        name="conformer_block",
    )(lengths, mel, route, first, second, kernel, lin_in, wq, wk, wv, wo, pw1)


def local(mel_in, route, lengths, conv_first, conv_second, lin_in, wq, wk, wv, wo, pw1, dw_kernel):
    encoded, _ = block(
        lengths, mel_in, route.reshape(SLOT, 128), conv_first, conv_second, dw_kernel,
        lin_in.reshape(16, 256, D), wq, wk, wv, wo, pw1,
    )
    return encoded[None]


def solution(mesh):
    return jax.shard_map(
        local,
        mesh=mesh,
        in_specs=(
            P(("ctx", "sess"), None),
            P(("ctx", "sess")),
            P(),
            P(),
            P(),
            P(),
            P("sess", None),
            P("sess", None),
            P("sess", None),
            P("sess", None),
            P("sess", None),
            P(),
        ),
        out_specs=P("sess", "ctx", None),
        check_vma=False,
    )
```

time: 155 us -> 127 us (0.82); the launches traced: 153 us -> 127 us
  Pallas kernels: 140 us -> 125 us
  local copies, waits for them, and re-layouts: 7.49 us -> 2.36 us
  other arithmetic: 4.59 us -> 0 us
    pallas_call x1, Pallas kernels: 140 us -> 125 us  [block(): pl.pallas_call(block_kernel, out_shape=[jax.ShapeDtypeStruct((ROWS, D), B...]
    concatenate x3 -> x0, other arithmetic: 4.12 us -> none  [the longest x1 1.9 us: local(): qkv_own = jnp.concatenate([wq, wk, wv], axis=1)]
    pad x2 -> x0, local copies, waits for them, and re-layouts: 2.83 us -> none  [the longest x1 1.55 us: local(): kernel = jnp.pad(dw_kernel, ((0, 1), (0, 0)))]
where the time goes in v3:
time: 127 us
  Pallas kernels  125 us (98%)
  local copies, waits for them, and re-layouts  2.36 us (2%)
    pallas_call x1, Pallas kernels, block(): pl.pallas_call(block_kernel, out_shape=[jax.ShapeDtypeStruct((ROWS, D), B...  125 us

profile of v3, /device:TPU:1, one launch (start us, length us, event | category | flops | bytes accessed | tf_op | source)
XLA Modules:
  0.0 127.1 jit_solution(1323488585495298768)
XLA Ops:
  0.0 124.7 %conformer_block.1 = (bf16[384,1536]{1,0:T(8,128)(2,1)}, bf16[16,240,1536]{2,1,0:T(8,128)(2,1)}) custom-call(s32[16]{0:T(128)} %lengths.1, bf16[1536,128]{1,0:T(8,128)(2,1)} %mel.1, s32[12,128]{1,0:T(8,128)} %bitcast.5, bf16[9,128]{1,0:T(8,128)(2,1)} %first.1, bf16[1152,128]{1,0:T(8,128)(2,1)} %second.1, bf16[31,1536]{1,0:T(8,128)(2,1)} %kernel.1, ...), custom_call_target="tpu_custom_call" | custom-call | flops 27000000512 | bytes 60000000 | tf_op jit(solution)/shard_map/conformer_block/pallas_call | solution.py:601
  124.7 2.4 %copy.14 = bf16[1,384,1536]{2,1,0:T(8,128)(2,1)} copy(bf16[1,384,1536]{2,1,0:T(8,128)(2,1)} %bitcast.3) | data formatting | bytes 2359296

commit v4 on v3

--- a/solution.py
+++ b/solution.py
@@ -251,16 +251,16 @@
     own_tail = pltpu.make_async_copy(tail_own, tail_full.at[sess], local_sem.at[3])
     own_tail.start()
     pl.semaphore_wait(barrier, RANKS - 1)
+
+    def deliver(i, carry):
+        other = lax.rem(me + i, RANKS)
+        remote(slots.at[other], arrived.at[me], mel_send, mel_recv, (other // 16, other % 16)).start()
+        return carry
+
+    lax.fori_loop(1, RANKS, deliver, 0)
     gather_k.start()
     gather_v.start()
     gather_q.start()
-
-    def deliver(i, carry):
-        other = lax.rem(me + i, RANKS)
-        remote(slots.at[other], arrived.at[me], mel_send, mel_recv, (other // 16, other % 16)).start()
-        return carry
-
-    lax.fori_loop(1, RANKS, deliver, 0)
     own_slot.wait()
     own_tail.wait()
     gather_t.begin()

time: 127 us -> 118 us (0.929)
  Pallas kernels: 125 us -> 116 us
    pallas_call x1, Pallas kernels: 125 us -> 116 us  [block(): pl.pallas_call(block_kernel, out_shape=[jax.ShapeDtypeStruct((ROWS, D), B...]
where the time goes in v4:
time: 118 us
  Pallas kernels  116 us (98%)
  local copies, waits for them, and re-layouts  2.36 us (2%)
    pallas_call x1, Pallas kernels, block(): pl.pallas_call(block_kernel, out_shape=[jax.ShapeDtypeStruct((ROWS, D), B...  116 us
    unnamed x1, local copies, waits for them, and re-layouts  2.36 us

profile of v4, /device:TPU:1, one launch (start us, length us, event | category | flops | bytes accessed | tf_op | source)
XLA Modules:
  0.0 118.0 jit_solution(6580385604402216020)
XLA Ops:
  0.0 115.6 %conformer_block.1 = (bf16[384,1536]{1,0:T(8,128)(2,1)}, bf16[16,240,1536]{2,1,0:T(8,128)(2,1)}) custom-call(s32[16]{0:T(128)} %lengths.1, bf16[1536,128]{1,0:T(8,128)(2,1)} %mel.1, s32[12,128]{1,0:T(8,128)} %bitcast.5, bf16[9,128]{1,0:T(8,128)(2,1)} %first.1, bf16[1152,128]{1,0:T(8,128)(2,1)} %second.1, bf16[31,1536]{1,0:T(8,128)(2,1)} %kernel.1, ...), custom_call_target="tpu_custom_call" | custom-call | flops 27000000512 | bytes 60000000 | tf_op jit(solution)/shard_map/conformer_block/pallas_call | solution.py:601
  115.6 2.4 %copy.14 = bf16[1,384,1536]{2,1,0:T(8,128)(2,1)} copy(bf16[1,384,1536]{2,1,0:T(8,128)(2,1)} %bitcast.3) | data formatting | bytes 2359296

commit v5 on v4

--- a/solution.py
+++ b/solution.py
@@ -24,6 +24,7 @@
 MESH = pl.DeviceIdType.MESH
 PARTS = 8
 HALF = ROWS // 2
+QUARTER = HALF // 4
 MIB = 1024 * 1024
 
 
@@ -194,10 +195,10 @@
     lengths, mel, route, first, second, kernel, lin_hbm, wq, wk, wv, wo, pw1,
     out, tail_full,
     mel_wide, high, low, slots, arrived, wide, turned, sorted_rows, frames, halo, last, sel, win_e, win_o,
-    band, taps, even, odd, behind, sub, big, emb, normed, w_q, w_k, w_v, sent, held, context, heads, tail_own,
+    band, taps, even, odd, behind, sub, big, emb, normed, w_q, w_k, w_v, packed, shares, packed_q, shares_q, held, context, heads, tail_own,
     residual, gated, edges, deep,
     mel_send, mel_recv, local_sem, halo_send, halo_recv,
-    qkv_send, qkv_recv, head_send, head_recv, edge_send, edge_recv, gather_send, gather_recv,
+    share_send, share_recv, query_send, query_recv, head_send, head_recv, edge_send, edge_recv, gather_send, gather_recv,
 ):
     ctx, sess = lax.axis_index("ctx"), lax.axis_index("sess")
     me = ctx * 16 + sess
@@ -288,8 +289,8 @@
         [lambda: gather_v.along_z(1), gather_t.start_other],
         [lambda: gather_q.along_z(1), gather_k.along_y],
         [gather_v.along_y],
+        [],
         [gather_q.along_y],
-        [gather_k.finish, gather_v.finish],
     ]
 
     def four_bins(g, side):
@@ -339,27 +340,13 @@
 
         @pl.when(half == 0)
         def _():
-            gather_q.finish()
-
-        lane = iota((HALF, 128), 1)
-        live = iota((HALF, 128), 0) < live_rows - start
-        for part, weights in ((1, w_k), (2, w_v), (0, w_q)):
+            gather_k.finish()
+            gather_v.finish()
+
+        for part, weights in ((0, w_k), (1, w_v)):
             rows = dot(normed[mine, :], merged(weights[...]))
-            if part == 1:
-                extra = jnp.where(live, 0.0, -1e30)
-            else:
-                extra = jnp.ones((HALF, 128), F32)
             for h in range(HEADS):
-                base, shift = (96 * h) // 128 * 128, (96 * h) % 128
-                if shift == 0:
-                    head = rows[:, base : base + 128]
-                elif shift == 32:
-                    head = pltpu.roll(rows[:, base : base + 128], 128 - shift, 1)
-                else:
-                    head = pltpu.roll(rows[:, base : base + 256], 256 - shift, 1)[:, 0:128]
-                head = jnp.where(lane < HEAD, head, jnp.where(lane == HEAD, extra, 0.0))
-                sent[part, h, mine] = head.astype(BF16)
-            own_share(half, part).start()
+                packed[part, half, h] = packed_head(rows, h)
 
             def share(i, carry):
                 share_of(half, part, i).start()
@@ -368,30 +355,57 @@
             lax.fori_loop(1, PARTS, share, 0)
         return carry
 
-    def own_share(half, part):
-        mine = pl.ds(pl.multiple_of(half * HALF, HALF), HALF)
-        return pltpu.make_async_copy(
-            sent.at[part, ctx, mine], held.at[part, ctx, mine], local_sem.at[8 + 3 * half + part]
-        )
-
     def share_of(half, part, i):
-        mine = pl.ds(pl.multiple_of(half * HALF, HALF), HALF)
         other = lax.rem(ctx + i, PARTS)
         return remote(
-            sent.at[part, other, mine], held.at[part, ctx, mine],
-            qkv_send.at[half, part, i], qkv_recv.at[half, part, i], (other, sess),
+            packed.at[part, half, other], shares.at[part, half, ctx],
+            share_send.at[half, part, i], share_recv.at[half, part, i], (other, sess),
         )
 
+    def queries_for(i):
+        other = lax.rem(ctx + i, PARTS)
+        return remote(
+            packed_q.at[other], shares_q.at[ctx], query_send.at[i], query_recv.at[i], (other, sess)
+        )
+
     lax.fori_loop(0, 2, rows_of, 0)
+    gather_q.finish()
+    for half in range(2):
+        rows = dot(normed[half * HALF : (half + 1) * HALF, :], merged(w_q[...]))
+        for h in range(HEADS):
+            packed_q[h, half] = packed_head(rows, h)
+    own_queries = pltpu.make_async_copy(packed_q.at[ctx], shares_q.at[ctx], local_sem.at[8])
+    own_queries.start()
+
+    def ask(i, carry):
+        queries_for(i).start()
+        return carry
+
+    lax.fori_loop(1, PARTS, ask, 0)
     gather_t.along_x(0)
+
+    def land(half, part, block, source):
+        def extra(row):
+            if part == 1:
+                return jnp.ones((QUARTER, 128), F32)
+            first_row = source * ROWS + half * HALF + row
+            live = iota((QUARTER, 128), 0) < lengths[sess] - first_row
+            return jnp.where(live, 0.0, -1e30)
+
+        for q, rows in enumerate(unpacked_head(block, extra)):
+            held[part, source, half * HALF + q * QUARTER : half * HALF + (q + 1) * QUARTER, :] = rows
+
     for half in range(2):
-        for part in range(3):
-            own_share(half, part).wait()
-    for part in (1, 2):
-        for half in range(2):
+        for part in range(2):
+            land(half, part, packed[part, half, ctx], ctx)
+    own_queries.wait()
+    for half in range(2):
+        for part in range(2):
 
             def arrive(i, carry):
                 share_of(half, part, i).wait_recv()
+                source = lax.rem(ctx + PARTS - i, PARTS)
+                land(half, part, shares[part, half, source], source)
                 return carry
 
             lax.fori_loop(1, PARTS, arrive, 0)
@@ -400,11 +414,13 @@
 
     def attend(i):
         other = lax.rem(ctx + PARTS - i, PARTS)
-        keys, values = merged(held[1]), merged(held[2])
+        keys, values = merged(held[0]), merged(held[1])
+        ones = lambda row: jnp.ones((QUARTER, 128), F32)
         for half in range(2):
             at = pl.ds(half * HALF, HALF)
+            queries = jnp.concatenate(unpacked_head(shares_q[other, half], ones), axis=0)
             scores = lax.dot_general(
-                held[0, other, at, :], keys, (((1,), (1,)), ((), ())), preferred_element_type=F32
+                queries, keys, (((1,), (1,)), ((), ())), preferred_element_type=F32
             )
             row_max = jnp.max(scores, axis=1, keepdims=True)
             weights = jnp.exp2((scores - row_max) * scale).astype(BF16)
@@ -430,8 +446,7 @@
     def attend_for(i, carry):
         @pl.when(i < PARTS)
         def _():
-            share_of(0, 0, i).wait_recv()
-            share_of(1, 0, i).wait_recv()
+            queries_for(i).wait_recv()
 
         attend(i)
 
@@ -520,15 +535,50 @@
     to_after.wait_send()
     to_before.wait_send()
     for half in range(2):
-        for part in range(3):
+        for part in range(2):
 
             def leave(i, carry):
                 share_of(half, part, i).wait_send()
                 return carry
 
             lax.fori_loop(1, PARTS, leave, 0)
+
+    def asked(i, carry):
+        queries_for(i).wait_send()
+        return carry
+
+    lax.fori_loop(1, PARTS, asked, 0)
     for gather in (gather_k, gather_v, gather_q, gather_t):
         gather.drain()
+
+
+def packed_head(rows, h):
+    base, shift = (HEAD * h) // 128 * 128, (HEAD * h) % 128
+    if shift == 0:
+        head = rows[:, base : base + 128]
+    elif shift == 32:
+        head = pltpu.roll(rows[:, base : base + 128], 128 - shift, 1)
+    else:
+        head = pltpu.roll(rows[:, base : base + 256], 256 - shift, 1)[:, 0:128]
+    lane = iota((QUARTER, 128), 1)
+    last = head[3 * QUARTER :]
+    quarters = [
+        jnp.where(lane < HEAD, head[q * QUARTER : (q + 1) * QUARTER], pltpu.roll(last, HEAD - 32 * q, 1))
+        for q in range(3)
+    ]
+    return jnp.concatenate(quarters, axis=0).astype(BF16)
+
+
+def unpacked_head(block, extra):
+    block = block.astype(F32)
+    quarters = [block[q * QUARTER : (q + 1) * QUARTER] for q in range(3)]
+    lane = iota((QUARTER, 128), 1)
+    pieces = [pltpu.roll(quarters[q], 32 * q + 32, 1) for q in range(3)]
+    quarters.append(jnp.where(lane < 32, pieces[0], jnp.where(lane < 64, pieces[1], pieces[2])))
+    return [
+        jnp.where(lane < HEAD, rows, jnp.where(lane == HEAD, extra(q * QUARTER), 0.0)).astype(BF16)
+        for q, rows in enumerate(quarters)
+    ]
 
 
 def pack_slots(mel, route, mel_wide, high, low, wide, slots):
@@ -633,8 +683,11 @@
             VMEM((16, 96, 768), BF16),
             VMEM((16, 96, 768), BF16),
             VMEM((16, 96, 768), BF16),
-            VMEM((3, HEADS, ROWS, 128), BF16),
-            VMEM((3, HEADS, ROWS, 128), BF16),
+            VMEM((2, 2, HEADS, 3 * QUARTER, 128), BF16),
+            VMEM((2, 2, PARTS, 3 * QUARTER, 128), BF16),
+            VMEM((HEADS, 2, 3 * QUARTER, 128), BF16),
+            VMEM((PARTS, 2, 3 * QUARTER, 128), BF16),
+            VMEM((2, PARTS, ROWS, 128), BF16),
             VMEM((HEADS, ROWS, 128), BF16),
             VMEM((HEADS, ROWS, 128), BF16),
             VMEM((240, D), BF16),
@@ -643,7 +696,8 @@
             VMEM((2, PAD, D), BF16),
             VMEM((D // 128, ROWS + 2 * PAD, 128), F32),
             DMA, DMA, DMA((16,)), DMA, DMA,
-            DMA((2, 3, PARTS)), DMA((2, 3, PARTS)), DMA((PARTS,)), DMA((PARTS,)), DMA((2,)), DMA((2,)),
+            DMA((2, 2, PARTS)), DMA((2, 2, PARTS)), DMA((PARTS,)), DMA((PARTS,)),
+            DMA((PARTS,)), DMA((PARTS,)), DMA((2,)), DMA((2,)),
             DMA((4, GATHER_SENDS)), DMA((4, GATHER_RECVS)),
         ],
         compiler_params=pltpu.CompilerParams(

time: 118 us -> 112 us (0.949)
  Pallas kernels: 116 us -> 109 us
    pallas_call x1, Pallas kernels: 116 us -> 109 us  [block(): pl.pallas_call(block_kernel, out_shape=[jax.ShapeDtypeStruct((ROWS, D), B...]
where the time goes in v5:
time: 112 us
  Pallas kernels  109 us (97%)
  local copies, waits for them, and re-layouts  2.36 us (2%)
    pallas_call x1, Pallas kernels, block(): pl.pallas_call(block_kernel, out_shape=[jax.ShapeDtypeStruct((ROWS, D), B...  109 us
    unnamed x1, local copies, waits for them, and re-layouts  2.36 us

profile of v5, /device:TPU:1, one launch (start us, length us, event | category | flops | bytes accessed | tf_op | source)
XLA Modules:
  0.0 111.7 jit_solution(743317969886280685)
XLA Ops:
  0.0 109.4 %conformer_block.1 = (bf16[384,1536]{1,0:T(8,128)(2,1)}, bf16[16,240,1536]{2,1,0:T(8,128)(2,1)}) custom-call(s32[16]{0:T(128)} %lengths.1, bf16[1536,128]{1,0:T(8,128)(2,1)} %mel.1, s32[12,128]{1,0:T(8,128)} %bitcast.5, bf16[9,128]{1,0:T(8,128)(2,1)} %first.1, bf16[1152,128]{1,0:T(8,128)(2,1)} %second.1, bf16[31,1536]{1,0:T(8,128)(2,1)} %kernel.1, ...), custom_call_target="tpu_custom_call" | custom-call | flops 27000000512 | bytes 60000000 | tf_op jit(solution)/shard_map/conformer_block/pallas_call | solution.py:651
  109.4 2.4 %copy.14 = bf16[1,384,1536]{2,1,0:T(8,128)(2,1)} copy(bf16[1,384,1536]{2,1,0:T(8,128)(2,1)} %bitcast.3) | data formatting | bytes 2359296
